TPU v7x, 32 devices: a whole 2x2x4 slice. The times are simulated.
32 devices in a mesh: group: 2 (over y), blk: 4 (over z), tensor: 4 (over x, core).
Axes of the slice: x: 2, y: 2, z: 4, core: 2. Of those that a mesh axis runs over, the one named last changes fastest.
Arguments:
- queries: bfloat16 [8, 256, 64, 128], P(('group', 'blk'), None, 'tensor'), parts along dimension 0, may hold values from -36 to 36
- new_kv: bfloat16 [2, 8, 256, 8, 128], P(None, ('group', 'blk'), None, 'tensor'), parts along dimension 1, may hold values from -24 to 24
- pool: bfloat16 [192, 2, 128, 8, 128], P(('group', 'blk'), None, None, 'tensor'), parts along dimension 0, may hold values from -6 to 6
- prefix_slot: int32 [8, 32], P(('group', 'blk')), parts along dimension 0, may hold values from 0 to 23
- prefix_owner: int32 [8, 32], P(('group', 'blk')), parts along dimension 0, may hold values from 0 to 3, as said below
- prefix_len: int32 [8], P(('group', 'blk')), parts along dimension 0, may hold values from 1 to 32, as said below
- write_slot: int32 [8, 2], P(('group', 'blk')), parts along dimension 0, may hold values from 0 to 23
- write_owner: int32 [8, 2], P(('group', 'blk')), parts along dimension 0, may hold values from 0 to 3, as said below
Outputs:
- attended: bfloat16 [8, 256, 64, 128], P(('group', 'blk'), None, 'tensor'), parts along dimension 0
- new_pool: bfloat16 [192, 2, 128, 8, 128], P(('group', 'blk'), None, None, 'tensor'), parts along dimension 0
There are 2 independent parts, one for each index of `group`. A program takes and returns all parts, laid end to end along the dimension named above; each array names one. Nothing has to cross between parts.
Inputs may be any that keep to these rules, and one draw needn't show every extreme that they name: `prefix_owner`: in the rows of one request no owner appears more than 8 times; some owner appears exactly 8 times in every request's row. `prefix_len`: some request has exactly 32 prefix blocks. `write_owner`: no two new blocks go to the same pool row; the new blocks of the requests of one index of blk go to different owners; every owner receives exactly 2 new blocks (the requests' new blocks spread evenly over the owners).
All inputs are finite; a program needn't handle non-finite values.
Results may differ from a plain program's by a relative error of at most 0.0065.
Values may be sent and summed in bfloat16 or wider, within the bound.
No kernel may reach another device: no remote copies, remote signals or barrier semaphores. Data moves between devices by JAX's collectives and lax.ppermute only.
A program may use at most 64 MiB of HBM per device.

v0:
```python
import functools
import math

import jax
import jax.numpy as jnp
from jax import lax
from jax.experimental import pallas as pl
from jax.experimental.pallas import tpu as pltpu
from jax.sharding import PartitionSpec as P

ANY = pl.BlockSpec(memory_space=pl.ANY)
HBM = pl.BlockSpec(memory_space=pltpu.HBM)
SMEM = pl.BlockSpec(memory_space=pltpu.SMEM)
VMEM = pl.BlockSpec(memory_space=pltpu.VMEM)
WHOLE_LIMIT = 60 * 1024 * 1024
VMEM_LIMIT = 16 * 1024 * 1024
ATTEND_LIMIT = 32 * 1024 * 1024
QUERY_ROWS = 1024
SAFE_ROWS = 256
HEADROOM = 60.0


def prepare_kernel(capacity, *refs):
    sources, refs = refs[:5], refs[5:]
    num_blk = refs[0].shape[1] // 2
    count_ref, asked, refs = refs[0], refs[1 : 1 + num_blk], refs[1 + num_blk :]
    held, (table_ref, used_ref, counted_ref, load_sems) = refs[:5], refs[5:]
    loads = [
        pltpu.make_async_copy(source, target, load_sems.at[i])
        for i, (source, target) in enumerate(zip(sources, held))
    ]
    for load in loads:
        load.start()
    slot_ref, owner_ref, len_ref, write_slot_ref, write_owner_ref = held
    me = lax.axis_index("blk")
    for owner in range(num_blk):
        used_ref[owner] = 0
        counted_ref[owner] = 0
        for k in range(capacity):
            table_ref[owner, k] = 0
    for load in loads:
        load.wait()

    def step(j, carry):
        owner = owner_ref[0, j]
        place = used_ref[owner]
        table_ref[owner, jnp.minimum(place, capacity)] = slot_ref[0, j]
        used_ref[owner] = place + 1
        counted_ref[owner] += jnp.where(j < len_ref[0], 1, 0)
        return carry

    lax.fori_loop(0, owner_ref.shape[1], step, 0, unroll=8)
    for d in range(num_blk):
        owner = lax.rem(me + d, num_blk)
        count_ref[0, d] = counted_ref[owner]
        for k in range(capacity):
            asked[d][0, k] = table_ref[owner, k]
        slot = jnp.int32(-1)
        chosen = jnp.int32(0)
        for b in range(write_owner_ref.shape[1]):
            goes = write_owner_ref[0, b] == owner
            slot = jnp.where(goes, write_slot_ref[0, b], slot)
            chosen = jnp.where(goes, b, chosen)
        asked[d][0, capacity] = slot
        count_ref[0, num_blk + d] = chosen


def prepare(prefix_slot, prefix_owner, prefix_len, write_slot, write_owner, capacity, num_blk):
    operands = (prefix_slot, prefix_owner, prefix_len, write_slot, write_owner)
    row = jax.ShapeDtypeStruct((1, capacity + 1), jnp.int32)
    results = pl.pallas_call(
        functools.partial(prepare_kernel, capacity),
        out_shape=[jax.ShapeDtypeStruct((1, 2 * num_blk), jnp.int32)] + [row] * num_blk,
        in_specs=[HBM] * 5,
        out_specs=[SMEM] * (num_blk + 1),
        scratch_shapes=[pltpu.SMEM(operand.shape, operand.dtype) for operand in operands]
        + [
            pltpu.SMEM((num_blk, capacity + 1), jnp.int32),
            pltpu.SMEM((num_blk,), jnp.int32),
            pltpu.SMEM((num_blk,), jnp.int32),
            pltpu.SemaphoreType.DMA((5,)),
        ],
        compiler_params=pltpu.CompilerParams(vmem_limit_bytes=WHOLE_LIMIT),
    )(*operands)
    return results[0], results[1:]


def gather_kernel(plan, count, block_rows, direct, whole, count_ref, *refs):
    asked, pool_ref, new_ref = refs[:count], refs[count], refs[count + 1]
    refs = refs[-len(plan) - whole - (1 if direct else 3) :]
    outs, refs = refs[: len(plan) + whole], refs[len(plan) + whole :]
    sems = refs[0]
    moves = []

    def move(source, target):
        i = len(moves)
        if direct:
            load, store = None, pltpu.make_async_copy(source, target, sems.at[i])
            store.start()
        else:
            held, in_sems = refs[1:]
            load = pltpu.make_async_copy(source, held.at[i], in_sems.at[i])
            store = pltpu.make_async_copy(held.at[i], target, sems.at[i])
            load.start()
        moves.append((load, store))

    for (row, start, size, to), out in zip(plan, outs):
        for place in range(size):
            move(pool_ref.at[asked[row][0, start + place]], out.at[place])
        if to is not None:
            chosen = count_ref[0, count_ref.shape[1] // 2 + to]
            at = pl.ds(pl.multiple_of(chosen * block_rows, block_rows), block_rows)
            move(new_ref.at[:, at], out.at[size])
    if whole:
        for b in range(pool_ref.shape[0]):
            move(pool_ref.at[b], outs[-1].at[b])
    if not direct:
        for load, store in moves:
            load.wait()
            store.start()
    for _, store in moves:
        store.wait()


def gather(counts, asked, pool, new_rows, plan, after=(), direct=True, whole=False):
    sizes = [size + (to is not None) for _, _, size, to in plan] + [pool.shape[0]] * whole
    blocks = sum(sizes)
    scratch = [pltpu.SemaphoreType.DMA((blocks,))]
    if not direct:
        scratch.append(pltpu.VMEM((blocks,) + pool.shape[1:], pool.dtype))
        scratch.append(pltpu.SemaphoreType.DMA((blocks,)))
    return pl.pallas_call(
        functools.partial(gather_kernel, plan, len(asked), pool.shape[2], direct, whole),
        out_shape=[jax.ShapeDtypeStruct((size,) + pool.shape[1:], pool.dtype) for size in sizes],
        in_specs=[SMEM] * (1 + len(asked)) + [VMEM if direct else HBM] * 2 + [ANY] * len(after),
        out_specs=[ANY if direct else HBM] * len(sizes),
        scratch_shapes=scratch,
        compiler_params=pltpu.CompilerParams(
            vmem_limit_bytes=VMEM_LIMIT if direct else WHOLE_LIMIT
        ),
        cost_estimate=pl.CostEstimate(
            flops=0, bytes_accessed=4 * blocks * math.prod(pool.shape[1:]), transcendentals=0
        ),
    )(counts, *asked, pool, new_rows, *after)


def write_back_kernel(capacity, block_rows, count, owner_ref, slot_ref, *refs):
    asked, refs = refs[:count], refs[count:]
    new_ref, fresh = refs[0], refs[1 : count + 1]
    out_ref, token_ref, sem = refs[count + 2 :]
    me = lax.axis_index("blk")
    token_ref[0, 0] = 0

    def put(wanted, src, slot):
        @pl.when(wanted)
        def write():
            copy = pltpu.make_async_copy(src, out_ref.at[slot], sem)
            copy.start()
            copy.wait()

    for i in range(count):
        slot = asked[i][0, capacity]
        put(slot >= 0, fresh[i].at[fresh[i].shape[0] - 1], slot)
    for b in range(owner_ref.shape[1]):
        rows = pl.ds(b * block_rows, block_rows)
        put(owner_ref[0, b] == me, new_ref.at[:, rows], slot_ref[0, b])


def write_back(write_owner, write_slot, asked, new_rows, fresh, pool, capacity):
    count = len(asked)
    return pl.pallas_call(
        functools.partial(write_back_kernel, capacity, pool.shape[2], count),
        out_shape=[
            jax.ShapeDtypeStruct(pool.shape, pool.dtype),
            jax.ShapeDtypeStruct((1, 1), jnp.int32),
        ],
        in_specs=[SMEM] * (count + 2) + [VMEM] * (count + 1) + [ANY],
        out_specs=[ANY, SMEM],
        scratch_shapes=[pltpu.SemaphoreType.DMA],
        input_output_aliases={2 * count + 3: 0},
        compiler_params=pltpu.CompilerParams(vmem_limit_bytes=VMEM_LIMIT),
        cost_estimate=pl.CostEstimate(flops=0, bytes_accessed=1 << 20, transcendentals=0),
    )(write_owner, write_slot, *asked, new_rows, *fresh, pool)


def attend_kernel(
    spans, relays, afters, kv_dev, group, block_tok, rows, first, final, count_ref, q_ref, *refs
):
    parts, refs = refs[: len(spans)], refs[len(spans) :]
    ins = 1 if first else 2
    outs = 1 if final else 3 if first else 2
    rest = refs[ins + relays + afters :]
    refs = refs[:ins] + rest[:outs] + rest[-3:]
    if first:
        new_ref, q_out, acc_out, stat_out = refs[:4]
        head_dim = q_ref.shape[2]
        suffix = new_ref.shape[1] // kv_dev
    else:
        acc_in, stat_in = refs[:2]
        head_dim = q_ref.shape[2]
        suffix = 0
        if final:
            out_ref = refs[2]
        else:
            acc_out, stat_out = refs[2:4]
    key_ref, value_ref, stage_ref = refs[-3:]
    factor = head_dim**-0.5 * math.log2(math.e)
    prefix_keys = sum(size for _, _, size in spans) * block_tok
    keys = prefix_keys + suffix

    def unpack(raw, kv, at):
        stage_ref[...] = raw.astype(jnp.float32)
        for h in range(kv_dev):
            head = stage_ref[pl.ds(h, block_tok, stride=kv_dev), :]
            if kv == 0:
                key_ref[h, pl.ds(at, block_tok)] = head.astype(jnp.bfloat16)
            else:
                value_ref[h, :head_dim, pl.ds(at, block_tok)] = head.T.astype(jnp.bfloat16)

    value_ref[:, head_dim:, :] = jnp.ones(
        (kv_dev, value_ref.shape[1] - head_dim, keys), jnp.bfloat16
    )
    base = 0
    for part, (row, start, size) in zip(parts, spans):
        for b in range(size):
            counts = count_ref[0, row] > start + b
            at = pl.ds(base + b * block_tok, block_tok)

            @pl.when(counts)
            def take(part=part, b=b, base=base):
                for kv in range(2):
                    unpack(part[b, kv], kv, base + b * block_tok)

            @pl.when(jnp.logical_not(counts))
            def leave_out(at=at):
                for h in range(kv_dev):
                    key_ref[h, at] = jnp.zeros((block_tok, head_dim), jnp.bfloat16)
                    value_ref[h, :, at] = jnp.zeros((value_ref.shape[1], block_tok), jnp.bfloat16)

        base += size * block_tok
    for piece in range(suffix // block_tok):
        for kv in range(2):
            raw = new_ref[kv, pl.ds(piece * block_tok * kv_dev, block_tok * kv_dev), :]
            unpack(raw, kv, base + piece * block_tok)

    if first:
        for h in range(kv_dev):
            heads = q_ref[...].astype(jnp.float32)[:, h * group : (h + 1) * group, :]
            q_out[h] = heads.reshape(-1, head_dim).astype(jnp.bfloat16)
        q_rows = q_out
    else:
        q_rows = q_ref

    def run(safe, rows):
        def product(start, stop, h, at):
            return lax.dot_general(
                key_ref[h, start:stop],
                q_rows[h, at],
                (((1,), (1,)), ((), ())),
                preferred_element_type=jnp.float32,
            )

        def sub(index, worst):
            at = pl.ds(pl.multiple_of(index * rows, rows), rows)
            results = []
            for h in range(kv_dev):
                pieces = []
                if spans:
                    scores = product(0, prefix_keys, h, at)
                    if first or safe:
                        place = lax.broadcasted_iota(jnp.int32, (prefix_keys, 1), 0)
                        allowed = jnp.zeros((prefix_keys, 1), jnp.bool_)
                        base = 0
                        for row, start, size in spans:
                            end = base + jnp.minimum(count_ref[0, row] - start, size) * block_tok
                            allowed |= (place >= base) & (place < end)
                            base += size * block_tok
                        scores = jnp.where(allowed, scores, -jnp.inf)
                    pieces.append((scores, 0))
                if first:
                    scores = product(prefix_keys, keys, h, at)
                    token = lax.broadcasted_iota(jnp.int32, (1, rows), 1) + index * rows
                    place = lax.broadcasted_iota(jnp.int32, (suffix, rows), 0)
                    scores = jnp.where(place * group <= token, scores, -jnp.inf)
                    pieces.append((scores, prefix_keys))
                peak = factor * functools.reduce(
                    jnp.maximum, [jnp.max(scores, axis=0, keepdims=True) for scores, _ in pieces]
                )
                if not first:
                    old = stat_in[h, 0:1, at]
                    if safe:
                        peak = jnp.maximum(peak, old)
                    else:
                        worst = jnp.maximum(worst, peak - old)
                        peak = old
                both = sum(
                    jnp.dot(
                        value_ref[h, :, start : start + scores.shape[0]],
                        jnp.exp2(scores * factor - peak).astype(jnp.bfloat16),
                        preferred_element_type=jnp.float32,
                    )
                    for scores, start in pieces
                )
                summed = both[:head_dim]
                total = both[head_dim : head_dim + 1]
                if not first:
                    shrink = jnp.exp2(old - peak) if safe else 1.0
                    summed += acc_in[h, :, at] * shrink
                    total += stat_in[h, 1:2, at] * shrink
                if final:
                    results.append((summed / total).T.reshape(rows // group, group, head_dim))
                else:
                    acc_out[h, :, at] = summed
                    stat_out[h, 0:1, at] = peak
                    stat_out[h, 1:2, at] = total
            if final:
                tok = pl.multiple_of(index * (rows // group), rows // group)
                out_ref[pl.ds(tok, rows // group)] = jnp.concatenate(results, axis=1).astype(
                    jnp.bfloat16
                )
            return worst

        worst = lax.fori_loop(
            0, q_rows.shape[1] // rows, sub, jnp.full((1, rows), -jnp.inf, jnp.float32)
        )
        if not first and not safe:

            @pl.when(jnp.max(worst) > HEADROOM)
            def again():
                run(True, min(rows, SAFE_ROWS))

    run(first, rows)


def attend(
    counts, queries, parts, spans, kv_dev, block_tok, new_rows=None, state=None, final=False, relay=(), after=()
):
    suffix, heads_dev, head_dim = queries.shape
    group = heads_dev // kv_dev
    first = state is None
    rows = min(QUERY_ROWS, suffix * group)
    keys = sum(size for _, _, size in spans) * block_tok + (suffix if first else 0)
    state_shape = [
        jax.ShapeDtypeStruct((kv_dev, suffix * group, head_dim), jnp.bfloat16),
        jax.ShapeDtypeStruct((kv_dev, head_dim, suffix * group), jnp.float32),
        jax.ShapeDtypeStruct((kv_dev, 8, suffix * group), jnp.float32),
    ]
    if first:
        operands = [queries, *parts, new_rows]
        out_shape = state_shape
    else:
        operands = [state[0], *parts, *state[1:]]
        out_shape = state_shape[1:]
        if final:
            out_shape = [jax.ShapeDtypeStruct(queries.shape, queries.dtype)]
    result = pl.pallas_call(
        functools.partial(
            attend_kernel, spans, len(relay), len(after), kv_dev, group, block_tok, rows, first, final
        ),
        out_shape=out_shape + [jax.ShapeDtypeStruct(x.shape, x.dtype) for x in relay],
        in_specs=[SMEM] + [VMEM] * len(operands) + [ANY] * (len(relay) + len(after)),
        out_specs=[VMEM] * len(out_shape) + [ANY] * len(relay),
        input_output_aliases={
            1 + len(operands) + i: len(out_shape) + i for i in range(len(relay))
        },
        scratch_shapes=[
            pltpu.VMEM((kv_dev, keys, head_dim), jnp.bfloat16),
            pltpu.VMEM((kv_dev, head_dim + 16, keys), jnp.bfloat16),
            pltpu.VMEM((block_tok * kv_dev, head_dim), jnp.float32),
        ],
        compiler_params=pltpu.CompilerParams(vmem_limit_bytes=ATTEND_LIMIT),
        cost_estimate=pl.CostEstimate(
            flops=4 * suffix * heads_dev * keys * head_dim,
            bytes_accessed=keys * kv_dev * head_dim * 4 + 16 * suffix * heads_dev * head_dim,
            transcendentals=suffix * heads_dev * keys,
        ),
    )(counts, *operands, *relay, *after)
    step, relayed = result[: len(out_shape)], result[len(out_shape) :]
    return (step if first or final else [state[0], *step]), relayed


def per_device(
    queries, new_kv, pool, prefix_slot, prefix_owner, prefix_len, write_slot, write_owner
):
    num_blk = lax.axis_size("blk")
    pool_dev, _, block_tok, kv_dev, head_dim = pool.shape
    suffix = queries.shape[1]
    prefix_blocks = prefix_slot.shape[1]
    capacity = max(2, (prefix_blocks + num_blk - 1) // num_blk)
    shifts = sorted(range(1, num_blk), key=lambda d: -min(d, num_blk - d))
    pool_rows = pool.reshape(pool_dev, 2, block_tok * kv_dev, head_dim)
    new_rows = new_kv.reshape(2, suffix * kv_dev, head_dim)

    def shift(array, d):
        return lax.ppermute(array, "blk", [(i, (i + d) % num_blk) for i in range(num_blk)])

    counts, asks = prepare(
        prefix_slot, prefix_owner, prefix_len, write_slot, write_owner, capacity, num_blk
    )
    asked = {d: shift(asks[d], d) for d in shifts}
    rows = [asked[d] for d in shifts]

    first = max(1, 3 * capacity // 8)
    cuts = sorted({0, first, 2 * first, capacity})
    plans = [[(d, start, end - start) for d in shifts] for start, end in zip(cuts, cuts[1:])]

    def load(plan, first, after=()):
        return gather(
            counts,
            rows,
            pool_rows,
            new_rows,
            tuple(
                (shifts.index(d), start, size, num_blk - d if first else None)
                for d, start, size in plan
            ),
            after,
            not first,
        )

    def send(plan, blocks):
        return [shift(x, num_blk - d) for (d, _, _), x in zip(plan, blocks)]

    loaded = load(plans[0], True)
    arrived = [send(plans[0], loaded)]
    local, new_pool = gather(
        counts, [asks[0]], pool_rows, new_rows, ((0, 0, capacity, None),), loaded[:1], whole=True
    )
    step = functools.partial(attend, counts, queries[0], kv_dev=kv_dev, block_tok=block_tok)
    state, _ = step([local], ((0, 0, capacity),), new_rows=new_rows)

    later = load(sum(plans[1:], []), False, [state[2]])
    arrived.append(send(plans[1], later[: len(shifts)]))
    token = None
    for i, plan in enumerate(plans):
        relay = later[len(shifts) :] if i == 0 else []
        groups = [slice(at, at + 8) for at in range(0, len(plan), 8)]
        for j, group in enumerate(groups):
            ends = j == len(groups) - 1
            state, relayed = step(
                arrived[i][group],
                tuple(plan[group]),
                state=state,
                final=ends and i == len(plans) - 1,
                relay=relay if ends else [],
                after=[token] if i == 1 and j == 0 else [],
            )
        if i == 0:
            for k in range(2, len(plans)):
                blocks, relayed = relayed[: len(plans[k])], relayed[len(plans[k]) :]
                arrived.append(send(plans[k], blocks))
            new_pool, token = write_back(
                write_owner,
                write_slot,
                [asked[num_blk - d] for d in shifts],
                new_rows,
                arrived[0],
                new_pool,
                capacity,
            )
    return state[0][None], new_pool.reshape(pool.shape)


def solution(mesh):
    in_specs = (
        P(("group", "blk"), None, "tensor", None),
        P(None, ("group", "blk"), None, "tensor", None),
        P(("group", "blk"), None, None, "tensor", None),
        P(("group", "blk"), None),
        P(("group", "blk"), None),
        P(("group", "blk")),
        P(("group", "blk"), None),
        P(("group", "blk"), None),
    )
    out_specs = (
        P(("group", "blk"), None, "tensor", None),
        P(("group", "blk"), None, None, "tensor", None),
    )
    return jax.shard_map(
        per_device, mesh=mesh, in_specs=in_specs, out_specs=out_specs, check_vma=False
    )
```

profile of v0, /device:TPU:14, one launch (start us, length us, event | category | flops | bytes accessed | tf_op | source)
XLA Modules:
  0.0 122.5 jit_solution(12651548527236021332)
XLA Ops:
  0.6 0.0 copy-start
  0.6 0.0 copy-start.1
  1.4 1.7 %shard_map.95 = (s32[1,8]{1,0:T(1,128)}, s32[1,9]{1,0:T(1,128)}, s32[1,9]{1,0:T(1,128)}, s32[1,9]{1,0:T(1,128)}, s32[1,9]{1,0:T(1,128)}) custom-call(s32[1,32]{1,0:T(1,128)} %refs_0_.1, s32[1,32]{1,0:T(1,128)} %refs_1_.1, s32[1]{0:T(128)S(6)} %copy.18.refs_2_, s32[1,2]{1,0:T(1,128)} %slot_ref.1, s32[1,2]{1,0:T(1,128)} %owner_ref.1), custom_call_target="tpu_custom_call" | custom-call | tf_op jit(solution)/shard_map/pallas_call | solution.py:71
  3.1 0.0 copy-start.3
  3.1 0.0 copy-start.12
  3.1 2.7 %collective-permute-start = (s32[1,9]{1,0:T(1,128)}, s32[1,9]{1,0:T(1,128)S(1)}, u32[]{:S(2)}, u32[]{:S(2)}) collective-permute-start(s32[1,9]{1,0:T(1,128)} %get-tuple-element.32), channel_id=1, source_target_pairs={{0,8},{4,12},{8,0},{12,4},{1,9},{5,13},{9,1},{13,5},{2,10},{6,14},... | collective-permute-start | bytes 116 | tf_op jit(solution)/shard_map/ppermute | solution.py:395
  5.8 0.0 collective-permute-start.1
  5.8 2.0 %collective-permute-start.2 = (s32[1,9]{1,0:T(1,128)}, s32[1,9]{1,0:T(1,128)S(1)}, u32[]{:S(2)}, u32[]{:S(2)}) collective-permute-start(s32[1,9]{1,0:T(1,128)} %get-tuple-element.34), channel_id=1, source_target_pairs={{0,12},{4,0},{8,4},{12,8},{1,13},{5,1},{9,5},{13,9},{2,14},{6,2},{... | collective-permute-start | bytes 116 | tf_op jit(solution)/shard_map/ppermute | solution.py:395
  7.8 0.0 collective-permute-done.refs_0_
  7.8 1.6 %collective-permute-done.1.refs_1_.refs_2_ = s32[1,9]{1,0:T(1,128)S(1)} collective-permute-done((s32[1,9]{1,0:T(1,128)}, s32[1,9]{1,0:T(1,128)S(1)}, u32[]{:S(2)}, u32[]{:S(2)}) %collective-permute-start.1) | collective-permute-done | bytes 68 | tf_op jit(solution)/shard_map/ppermute | solution.py:395
  9.5 0.0 collective-permute-done.2.refs_2_.refs_1_
  9.5 0.0 copy-done.4
  9.5 0.5 copy-done.6
  10.0 0.1 copy-done.8
  10.1 3.2 %shard_map.96 = (bf16[4,2,256,128]{3,2,1,0:T(8,128)(2,1)}, bf16[4,2,256,128]{3,2,1,0:T(8,128)(2,1)}, bf16[4,2,256,128]{3,2,1,0:T(8,128)(2,1)}) custom-call(s32[1,8]{1,0:T(1,128)} %get-tuple-element.30.count_ref, s32[1,9]{1,0:T(1,128)} %copy-done.4, s32[1,9]{1,0:T(1,128)} %copy-done.6, s32[1,9]{1,0:T(1,128)} %copy-done.8, bf16[24,2,256,128]{3,2,1,0:T(8,128)(2,1)} %bitcast.5, ...), custom_call_target="tpu_custom_call" | custom-call | bytes 3145728 | tf_op jit(solution)/shard_map/pallas_call | solution.py:132
  13.3 4.4 %collective-permute-start.3 = (bf16[4,2,256,128]{3,2,1,0:T(8,128)(2,1)}, bf16[4,2,256,128]{3,2,1,0:T(8,128)(2,1)S(1)}, u32[]{:S(2)}, u32[]{:S(2)}) collective-permute-start(bf16[4,2,256,128]{3,2,1,0:T(8,128)(2,1)} %get-tuple-element.35.refs_3_), channel_id=1, source_target_pairs={{0,8},{4,12},{8,0},{12,4},{1,9},{5,13},{9,1},{13,5},{2,10},{6,14},... | collective-permute-start | bytes 1572872 | tf_op jit(solution)/shard_map/ppermute | solution.py:395
  17.7 0.0 collective-permute-start.4
  17.7 2.0 %collective-permute-start.5 = (bf16[4,2,256,128]{3,2,1,0:T(8,128)(2,1)}, bf16[4,2,256,128]{3,2,1,0:T(8,128)(2,1)S(1)}, u32[]{:S(2)}, u32[]{:S(2)}) collective-permute-start(bf16[4,2,256,128]{3,2,1,0:T(8,128)(2,1)} %get-tuple-element.39), channel_id=1, source_target_pairs={{0,4},{4,8},{8,12},{12,0},{1,5},{5,9},{9,13},{13,1},{2,6},{6,10},{... | collective-permute-start | bytes 1572872 | tf_op jit(solution)/shard_map/ppermute | solution.py:395
  19.7 0.0 copy-done
  19.7 0.0 copy-done.1
  19.7 0.0 copy-done.3
  19.7 0.0 copy-done.12
  19.7 0.0 copy-start.2
  19.7 1.0 copy-done.2
  20.8 3.8 %shard_map.97 = (bf16[8,2,256,128]{3,2,1,0:T(8,128)(2,1)S(1)}, bf16[24,2,256,128]{3,2,1,0:T(8,128)(2,1)}) custom-call(s32[1,8]{1,0:T(1,128)S(1)} %copy-done.3, s32[1,9]{1,0:T(1,128)S(1)} %copy-done.12, bf16[24,2,256,128]{3,2,1,0:T(8,128)(2,1)S(1)} %bitcast.6, bf16[2,512,128]{2,1,0:T(8,128)(2,1)S(1)} %bitcast.9, bf16[4,2,256,128]{3,2,1,0:T(8,128)(2,1)S(1)} %copy-done.2), custom_call_target="tpu_custom_call" | custom-call | bytes 8388608 | tf_op jit(solution)/shard_map/pallas_call | solution.py:132
  24.6 0.0 copy-done.13
  24.7 9.3 %shard_map.98 = (bf16[2,2048,128]{2,1,0:T(8,128)(2,1)S(1)}, f32[2,128,2048]{2,1,0:T(8,128)S(1)}, f32[2,8,2048]{2,1,0:T(8,128)S(1)}) custom-call(s32[1,8]{1,0:T(1,128)S(1)} %copy-done.3, bf16[256,16,128]{2,1,0:T(8,128)(2,1)S(1)} %bitcast.13, bf16[8,2,256,128]{3,2,1,0:T(8,128)(2,1)S(1)} %get-tuple-element.36.refs_0_, bf16[2,512,128]{2,1,0:T(8,128)(2,1)S(1)} %bitcast.10), custom_call_target="tpu_custom_call" | custom-call | flops 2684354560 | bytes 9699328 | tf_op jit(solution)/shard_map/pallas_call | solution.py:356
  34.0 3.3 %shard_map.99 = (bf16[3,2,256,128]{3,2,1,0:T(8,128)(2,1)S(1)}, bf16[3,2,256,128]{3,2,1,0:T(8,128)(2,1)S(1)}, bf16[3,2,256,128]{3,2,1,0:T(8,128)(2,1)S(1)}, bf16[...) custom-call(s32[1,8]{1,0:T(1,128)S(1)} %copy-done.3, ...), custom_call_target="tpu_custom_call" | custom-call | bytes 3932160 | tf_op jit(solution)/shard_map/pallas_call | solution.py:132
  37.3 1.7 %collective-permute-start.9 = (bf16[3,2,256,128]{3,2,1,0:T(8,128)(2,1)S(1)}, bf16[3,2,256,128]{3,2,1,0:T(8,128)(2,1)S(1)}, u32[]{:S(2)}, u32[]{:S(2)}) collective-permute-start(bf16[3,2,256,128]{3,2,1,0:T(8,128)(2,1)S(1)} %get-tuple-element.48), channel_id=1, source_target_pairs={{0,8},{4,12},{8,0},{12,4},{1,9},{5,13},{9,1},{13,5},{2,10},{6,14},... | collective-permute-start | bytes 1179656 | tf_op jit(solution)/shard_map/ppermute | solution.py:395
  39.0 0.2 collective-permute-start.10
  39.2 11.6 %collective-permute-done.3.refs_0_.refs_4_ = bf16[4,2,256,128]{3,2,1,0:T(8,128)(2,1)S(1)} collective-permute-done((bf16[4,2,256,128]{3,2,1,0:T(8,128)(2,1)}, bf16[4,2,256,128]{3,2,1,0:T(8,128)(2,1)S(1)}, u32[]{:S(2)}, u32[]{:S(2)}) %collective-permute-start.3) | collective-permute-done | bytes 524320 | tf_op jit(solution)/shard_map/ppermute | solution.py:395
  50.8 0.0 collective-permute-start.11
  50.8 28.2 %collective-permute-done.4.refs_1_.refs_5_ = bf16[4,2,256,128]{3,2,1,0:T(8,128)(2,1)S(1)} collective-permute-done((bf16[4,2,256,128]{3,2,1,0:T(8,128)(2,1)}, bf16[4,2,256,128]{3,2,1,0:T(8,128)(2,1)S(1)}, u32[]{:S(2)}, u32[]{:S(2)}) %collective-permute-start.4) | collective-permute-done | bytes 524320 | tf_op jit(solution)/shard_map/ppermute | solution.py:395
  79.0 0.0 collective-permute-done.5.refs_2_.refs_6_
  79.0 6.3 %shard_map.100 = (f32[2,128,2048]{2,1,0:T(8,128)S(1)}, f32[2,8,2048]{2,1,0:T(8,128)S(1)}, bf16[2,2,256,128]{3,2,1,0:T(8,128)(2,1)S(1)}, bf16[2,2,256,128]{3,2,1,0:T(8,128)(2,1)S(1)}, bf16[2,2,256,128]{3,2,1,0:T(8,128)(2,1)S(1)}) custom-call(s32[1,8]{1,0:T(1,128)S(1)} %copy-done.3, ...), custom_call_target="tpu_custom_call", output_to_operand_aliasing={{2}: (7, {}), {3}: (8, {}), {4}: (9, {})} | custom-call | flops 2415919104 | bytes 9568256 | tf_op jit(solution)/shard_map/pallas_call | solution.py:356
  85.4 0.1 collective-permute-start.6
  85.5 1.6 %collective-permute-start.7 = (bf16[2,2,256,128]{3,2,1,0:T(8,128)(2,1)S(1)}, bf16[2,2,256,128]{3,2,1,0:T(8,128)(2,1)S(1)}, u32[]{:S(2)}, u32[]{:S(2)}) collective-permute-start(bf16[2,2,256,128]{3,2,1,0:T(8,128)(2,1)S(1)} %get-tuple-element.46), channel_id=1, source_target_pairs={{0,12},{4,0},{8,4},{12,8},{1,13},{5,1},{9,5},{13,9},{2,14},{6,2},{... | collective-permute-start | bytes 786440 | tf_op jit(solution)/shard_map/ppermute | solution.py:395
  87.1 0.0 collective-permute-done.9.refs_0_
  87.1 2.6 %collective-permute-start.8 = (bf16[2,2,256,128]{3,2,1,0:T(8,128)(2,1)S(1)}, bf16[2,2,256,128]{3,2,1,0:T(8,128)(2,1)S(1)}, u32[]{:S(2)}, u32[]{:S(2)}) collective-permute-start(bf16[2,2,256,128]{3,2,1,0:T(8,128)(2,1)S(1)} %get-tuple-element.47), channel_id=1, source_target_pairs={{0,4},{4,8},{8,12},{12,0},{1,5},{5,9},{9,13},{13,1},{2,6},{6,10},{... | collective-permute-start | bytes 786440 | tf_op jit(solution)/shard_map/ppermute | solution.py:395
  89.7 0.0 copy-done.11
  89.7 2.4 %shard_map.101 = (bf16[24,2,256,128]{3,2,1,0:T(8,128)(2,1)}, s32[1,1]{1,0:T(1,128)}) custom-call(s32[1,2]{1,0:T(1,128)S(1)} %copy-done.11, s32[1,2]{1,0:T(1,128)S(1)} %copy-done.10, s32[1,9]{1,0:T(1,128)S(1)} %copy-done.5, s32[1,9]{1,0:T(1,128)S(1)} %copy-done.9, s32[1,9]{1,0:T(1,128)S(1)} %copy-done.7, ...), custom_call_target="tpu_custom_call", output_to_operand_aliasing={{0}: (9, {})} | custom-call | bytes 1048576 | tf_op jit(solution)/shard_map/pallas_call | solution.py:171
  92.1 15.0 %collective-permute-done.10.refs_1_ = bf16[3,2,256,128]{3,2,1,0:T(8,128)(2,1)S(1)} collective-permute-done((bf16[3,2,256,128]{3,2,1,0:T(8,128)(2,1)S(1)}, bf16[3,2,256,128]{3,2,1,0:T(8,128)(2,1)S(1)}, u32[]{:S(2)}, u32[]{:S(2)}) %collective-permute-start.10) | collective-permute-done | bytes 393248 | tf_op jit(solution)/shard_map/ppermute | solution.py:395
  107.1 0.0 collective-permute-done.11.refs_2_
  107.1 6.8 %shard_map.102 = (f32[2,128,2048]{2,1,0:T(8,128)S(1)}, f32[2,8,2048]{2,1,0:T(8,128)S(1)}) custom-call(s32[1,8]{1,0:T(1,128)S(1)} %copy-done.3, bf16[2,2048,128]{2,1,0:T(8,128)(2,1)S(1)} %get-tuple-element.37.q_ref, bf16[3,2,256,128]{3,2,1,0:T(8,128)(2,1)S(1)} %collective-permute-done.9.refs_0_, bf16[3,2,256,128]{3,2,1,0:T(8,128)(2,1)S(1)} %collective-permute-done.10.refs_1_, ...), custom_call_target="tpu_custom_call" | custom-call | flops 2415919104 | bytes 9568256 | tf_op jit(solution)/shard_map/pallas_call | solution.py:356
  113.9 0.0 collective-permute-done.6.refs_0_
  113.9 3.3 %collective-permute-done.7.refs_1_ = bf16[2,2,256,128]{3,2,1,0:T(8,128)(2,1)S(1)} collective-permute-done((bf16[2,2,256,128]{3,2,1,0:T(8,128)(2,1)S(1)}, bf16[2,2,256,128]{3,2,1,0:T(8,128)(2,1)S(1)}, u32[]{:S(2)}, u32[]{:S(2)}) %collective-permute-start.7) | collective-permute-done | bytes 262176 | tf_op jit(solution)/shard_map/ppermute | solution.py:395
  117.2 0.0 collective-permute-done.8.refs_2_
  117.2 5.3 %shard_map.103 = bf16[256,16,128]{2,1,0:T(8,128)(2,1)} custom-call(s32[1,8]{1,0:T(1,128)S(1)} %copy-done.3, bf16[2,2048,128]{2,1,0:T(8,128)(2,1)S(1)} %get-tuple-element.37.q_ref, bf16[2,2,256,128]{3,2,1,0:T(8,128)(2,1)S(1)} %collective-permute-done.6.refs_0_, bf16[2,2,256,128]{3,2,1,0:T(8,128)(2,1)S(1)} %collective-permute-done.7.refs_1_, ...), custom_call_target="tpu_custom_call" | custom-call | flops 1610612736 | bytes 9175040 | tf_op jit(solution)/shard_map/pallas_call | solution.py:356
  (13 shorter events, 0.0 us)
Async XLA Ops:
  0.6 19.1 %copy-start = (bf16[24,2,128,2,128]{4,3,2,1,0:T(2,128)(2,1)S(1)}, bf16[24,2,128,2,128]{4,3,2,1,0:T(2,128)(2,1)}, u32[]{:S(2)}) copy-start(bf16[24,2,128,2,128]{4,3,2,1,0:T(2,128)(2,1)} %param.10) | copy-start | bytes 9437188
  0.6 19.1 %copy-start.1 = (bf16[2,1,256,2,128]{4,3,2,1,0:T(2,128)(2,1)S(1)}, bf16[2,1,256,2,128]{4,3,2,1,0:T(2,128)(2,1)}, u32[]{:S(2)}) copy-start(bf16[2,1,256,2,128]{4,3,2,1,0:T(2,128)(2,1)} %param.9) | copy-start | bytes 786436
  3.1 16.6 %copy-start.3 = (s32[1,8]{1,0:T(1,128)S(1)}, s32[1,8]{1,0:T(1,128)}, u32[]{:S(2)}) copy-start(s32[1,8]{1,0:T(1,128)} %get-tuple-element.30.count_ref) | copy-start | bytes 100
  3.1 16.6 %copy-start.12 = (s32[1,9]{1,0:T(1,128)S(1)}, s32[1,9]{1,0:T(1,128)}, u32[]{:S(2)}) copy-start(s32[1,9]{1,0:T(1,128)} %get-tuple-element.31.refs_0_) | copy-start | bytes 112
  3.1 4.7 %collective-permute-start = (s32[1,9]{1,0:T(1,128)}, s32[1,9]{1,0:T(1,128)S(1)}, u32[]{:S(2)}, u32[]{:S(2)}) collective-permute-start(s32[1,9]{1,0:T(1,128)} %get-tuple-element.32), channel_id=1, source_target_pairs={{0,8},{4,12},{8,0},{12,4},{1,9},{5,13},{9,1},{13,5},{2,10},{6,14},... | collective-permute-start | bytes 116 | tf_op jit(solution)/shard_map/ppermute | solution.py:395
  5.8 3.7 %collective-permute-start.1 = (s32[1,9]{1,0:T(1,128)}, s32[1,9]{1,0:T(1,128)S(1)}, u32[]{:S(2)}, u32[]{:S(2)}) collective-permute-start(s32[1,9]{1,0:T(1,128)} %get-tuple-element.33), channel_id=1, source_target_pairs={{0,4},{4,8},{8,12},{12,0},{1,5},{5,9},{9,13},{13,1},{2,6},{6,10},{... | collective-permute-start | bytes 116 | tf_op jit(solution)/shard_map/ppermute | solution.py:395
  5.8 3.7 %collective-permute-start.2 = (s32[1,9]{1,0:T(1,128)}, s32[1,9]{1,0:T(1,128)S(1)}, u32[]{:S(2)}, u32[]{:S(2)}) collective-permute-start(s32[1,9]{1,0:T(1,128)} %get-tuple-element.34), channel_id=1, source_target_pairs={{0,12},{4,0},{8,4},{12,8},{1,13},{5,1},{9,5},{13,9},{2,14},{6,2},{... | collective-permute-start | bytes 116 | tf_op jit(solution)/shard_map/ppermute | solution.py:395
  7.8 1.7 %copy-start.4 = (s32[1,9]{1,0:T(1,128)}, s32[1,9]{1,0:T(1,128)S(1)}, u32[]{:S(2)}) copy-start(s32[1,9]{1,0:T(1,128)S(1)} %collective-permute-done.refs_0_) | copy-start | bytes 112
  9.5 0.5 copy-start.6
  9.5 0.6 copy-start.8
  13.3 37.5 %collective-permute-start.3 = (bf16[4,2,256,128]{3,2,1,0:T(8,128)(2,1)}, bf16[4,2,256,128]{3,2,1,0:T(8,128)(2,1)S(1)}, u32[]{:S(2)}, u32[]{:S(2)}) collective-permute-start(bf16[4,2,256,128]{3,2,1,0:T(8,128)(2,1)} %get-tuple-element.35.refs_3_), channel_id=1, source_target_pairs={{0,8},{4,12},{8,0},{12,4},{1,9},{5,13},{9,1},{13,5},{2,10},{6,14},... | collective-permute-start | bytes 1572872 | tf_op jit(solution)/shard_map/ppermute | solution.py:395
  17.7 61.3 %collective-permute-start.4 = (bf16[4,2,256,128]{3,2,1,0:T(8,128)(2,1)}, bf16[4,2,256,128]{3,2,1,0:T(8,128)(2,1)S(1)}, u32[]{:S(2)}, u32[]{:S(2)}) collective-permute-start(bf16[4,2,256,128]{3,2,1,0:T(8,128)(2,1)} %get-tuple-element.38), channel_id=1, source_target_pairs={{0,12},{4,0},{8,4},{12,8},{1,13},{5,1},{9,5},{13,9},{2,14},{6,2},{... | collective-permute-start | bytes 1572872 | tf_op jit(solution)/shard_map/ppermute | solution.py:395
  17.7 61.3 %collective-permute-start.5 = (bf16[4,2,256,128]{3,2,1,0:T(8,128)(2,1)}, bf16[4,2,256,128]{3,2,1,0:T(8,128)(2,1)S(1)}, u32[]{:S(2)}, u32[]{:S(2)}) collective-permute-start(bf16[4,2,256,128]{3,2,1,0:T(8,128)(2,1)} %get-tuple-element.39), channel_id=1, source_target_pairs={{0,4},{4,8},{8,12},{12,0},{1,5},{5,9},{9,13},{13,1},{2,6},{6,10},{... | collective-permute-start | bytes 1572872 | tf_op jit(solution)/shard_map/ppermute | solution.py:395
  19.7 1.0 copy-start.2
  20.8 3.9 %copy-start.13 = (bf16[1,256,16,128]{3,2,1,0:T(8,128)(2,1)S(1)}, bf16[1,256,16,128]{3,2,1,0:T(8,128)(2,1)}, u32[]{:S(2)}) copy-start(bf16[1,256,16,128]{3,2,1,0:T(8,128)(2,1)} %param.8) | copy-start | bytes 3145732
  24.6 9.3 %copy-start.5 = (s32[1,9]{1,0:T(1,128)S(1)}, s32[1,9]{1,0:T(1,128)}, u32[]{:S(2)}) copy-start(s32[1,9]{1,0:T(1,128)} %copy-done.4) | copy-start | bytes 112
  24.6 9.3 %copy-start.7 = (s32[1,9]{1,0:T(1,128)S(1)}, s32[1,9]{1,0:T(1,128)}, u32[]{:S(2)}) copy-start(s32[1,9]{1,0:T(1,128)} %copy-done.6) | copy-start | bytes 112
  24.7 9.3 %copy-start.9 = (s32[1,9]{1,0:T(1,128)S(1)}, s32[1,9]{1,0:T(1,128)}, u32[]{:S(2)}) copy-start(s32[1,9]{1,0:T(1,128)} %copy-done.8) | copy-start | bytes 112
  37.3 49.8 %collective-permute-start.9 = (bf16[3,2,256,128]{3,2,1,0:T(8,128)(2,1)S(1)}, bf16[3,2,256,128]{3,2,1,0:T(8,128)(2,1)S(1)}, u32[]{:S(2)}, u32[]{:S(2)}) collective-permute-start(bf16[3,2,256,128]{3,2,1,0:T(8,128)(2,1)S(1)} %get-tuple-element.48), channel_id=1, source_target_pairs={{0,8},{4,12},{8,0},{12,4},{1,9},{5,13},{9,1},{13,5},{2,10},{6,14},... | collective-permute-start | bytes 1179656 | tf_op jit(solution)/shard_map/ppermute | solution.py:395
  39.0 68.1 %collective-permute-start.10 = (bf16[3,2,256,128]{3,2,1,0:T(8,128)(2,1)S(1)}, bf16[3,2,256,128]{3,2,1,0:T(8,128)(2,1)S(1)}, u32[]{:S(2)}, u32[]{:S(2)}) collective-permute-start(bf16[3,2,256,128]{3,2,1,0:T(8,128)(2,1)S(1)} %get-tuple-element.49), channel_id=1, source_target_pairs={{0,12},{4,0},{8,4},{12,8},{1,13},{5,1},{9,5},{13,9},{2,14},{6,2},{... | collective-permute-start | bytes 1179656 | tf_op jit(solution)/shard_map/ppermute | solution.py:395
  50.8 56.3 %collective-permute-start.11 = (bf16[3,2,256,128]{3,2,1,0:T(8,128)(2,1)S(1)}, bf16[3,2,256,128]{3,2,1,0:T(8,128)(2,1)S(1)}, u32[]{:S(2)}, u32[]{:S(2)}) collective-permute-start(bf16[3,2,256,128]{3,2,1,0:T(8,128)(2,1)S(1)} %get-tuple-element.50), channel_id=1, source_target_pairs={{0,4},{4,8},{8,12},{12,0},{1,5},{5,9},{9,13},{13,1},{2,6},{6,10},{... | collective-permute-start | bytes 1179656 | tf_op jit(solution)/shard_map/ppermute | solution.py:395
  79.0 10.6 %copy-start.10 = (s32[1,2]{1,0:T(1,128)S(1)}, s32[1,2]{1,0:T(1,128)}, u32[]{:S(2)}) copy-start(s32[1,2]{1,0:T(1,128)} %slot_ref.1) | copy-start | bytes 28
  79.0 10.6 %copy-start.11 = (s32[1,2]{1,0:T(1,128)S(1)}, s32[1,2]{1,0:T(1,128)}, u32[]{:S(2)}) copy-start(s32[1,2]{1,0:T(1,128)} %owner_ref.1) | copy-start | bytes 28
  85.4 28.5 %collective-permute-start.6 = (bf16[2,2,256,128]{3,2,1,0:T(8,128)(2,1)S(1)}, bf16[2,2,256,128]{3,2,1,0:T(8,128)(2,1)S(1)}, u32[]{:S(2)}, u32[]{:S(2)}) collective-permute-start(bf16[2,2,256,128]{3,2,1,0:T(8,128)(2,1)S(1)} %get-tuple-element.45), channel_id=1, source_target_pairs={{0,8},{4,12},{8,0},{12,4},{1,9},{5,13},{9,1},{13,5},{2,10},{6,14},... | collective-permute-start | bytes 786440 | tf_op jit(solution)/shard_map/ppermute | solution.py:395
  85.5 31.8 %collective-permute-start.7 = (bf16[2,2,256,128]{3,2,1,0:T(8,128)(2,1)S(1)}, bf16[2,2,256,128]{3,2,1,0:T(8,128)(2,1)S(1)}, u32[]{:S(2)}, u32[]{:S(2)}) collective-permute-start(bf16[2,2,256,128]{3,2,1,0:T(8,128)(2,1)S(1)} %get-tuple-element.46), channel_id=1, source_target_pairs={{0,12},{4,0},{8,4},{12,8},{1,13},{5,1},{9,5},{13,9},{2,14},{6,2},{... | collective-permute-start | bytes 786440 | tf_op jit(solution)/shard_map/ppermute | solution.py:395
  87.1 30.1 %collective-permute-start.8 = (bf16[2,2,256,128]{3,2,1,0:T(8,128)(2,1)S(1)}, bf16[2,2,256,128]{3,2,1,0:T(8,128)(2,1)S(1)}, u32[]{:S(2)}, u32[]{:S(2)}) collective-permute-start(bf16[2,2,256,128]{3,2,1,0:T(8,128)(2,1)S(1)} %get-tuple-element.47), channel_id=1, source_target_pairs={{0,4},{4,8},{8,12},{12,0},{1,5},{5,9},{9,13},{13,1},{2,6},{6,10},{... | collective-permute-start | bytes 786440 | tf_op jit(solution)/shard_map/ppermute | solution.py:395
where the time goes:
time: 123 us; the launch traced here: 122 us
  waiting for transfers between devices  59.8 us (49%)
  Pallas kernels  42.1 us (34%)
  starting transfers between devices  17.3 us (14%)
  local copies, waits for them, and re-layouts  1.68 us (1%)
  between operations  1.63 us (1%)
    ppermute x12, waiting for transfers between devices, shift(): lax.ppermute(array, 'blk', [(i, (i + d) % num_blk) for i in range(num_blk)])  59.8 us
    pallas_call x4, Pallas kernels, attend(): pl.pallas_call(functools.partial(attend_kernel, spans, len(relay), len(af...  27.6 us
    ppermute x12, starting transfers between devices, shift(): lax.ppermute(array, 'blk', [(i, (i + d) % num_blk) for i in range(num_blk)])  17.3 us
    pallas_call x3, Pallas kernels, gather(): pl.pallas_call(functools.partial(gather_kernel, plan, len(asked), pool.sh...  10.4 us
  transfers between devices with their start and end apart: 12, of which 5 were waited for; matrix products, arithmetic and copies ran while one was open for 0% of the time, Pallas kernels for 26%

commit v1 on v0

--- a/solution.py
+++ b/solution.py
@@ -20,18 +20,19 @@
 HEADROOM = 60.0
 
 
-def prepare_kernel(capacity, *refs):
-    sources, refs = refs[:5], refs[5:]
+def prepare_kernel(capacity, to, *refs):
+    sources, refs = refs[:6], refs[6:]
     num_blk = refs[0].shape[1] // 2
     count_ref, asked, refs = refs[0], refs[1 : 1 + num_blk], refs[1 + num_blk :]
-    held, (table_ref, used_ref, counted_ref, load_sems) = refs[:5], refs[5:]
+    fresh_ref, refs = refs[0], refs[1:]
+    held, (table_ref, used_ref, counted_ref, load_sems, store_sem) = refs[:6], refs[6:]
     loads = [
         pltpu.make_async_copy(source, target, load_sems.at[i])
         for i, (source, target) in enumerate(zip(sources, held))
     ]
     for load in loads:
         load.start()
-    slot_ref, owner_ref, len_ref, write_slot_ref, write_owner_ref = held
+    slot_ref, owner_ref, len_ref, write_slot_ref, write_owner_ref, new_ref = held
     me = lax.axis_index("blk")
     for owner in range(num_blk):
         used_ref[owner] = 0
@@ -40,6 +41,14 @@
             table_ref[owner, k] = 0
     for load in loads:
         load.wait()
+    target = lax.rem(me + to, num_blk)
+    chosen = jnp.int32(0)
+    for b in range(write_owner_ref.shape[1]):
+        chosen = jnp.where(write_owner_ref[0, b] == target, b, chosen)
+    block_rows = fresh_ref.shape[2]
+    rows = pl.ds(pl.multiple_of(chosen * block_rows, block_rows), block_rows)
+    store = pltpu.make_async_copy(new_ref.at[:, rows], fresh_ref.at[0], store_sem)
+    store.start()
 
     def step(j, carry):
         owner = owner_ref[0, j]
@@ -63,26 +72,35 @@
             chosen = jnp.where(goes, b, chosen)
         asked[d][0, capacity] = slot
         count_ref[0, num_blk + d] = chosen
-
-
-def prepare(prefix_slot, prefix_owner, prefix_len, write_slot, write_owner, capacity, num_blk):
-    operands = (prefix_slot, prefix_owner, prefix_len, write_slot, write_owner)
+    store.wait()
+
+
+def prepare(
+    prefix_slot, prefix_owner, prefix_len, write_slot, write_owner, new_rows, block_rows, to,
+    capacity, num_blk,
+):
+    operands = (prefix_slot, prefix_owner, prefix_len, write_slot, write_owner, new_rows)
+    block = jax.ShapeDtypeStruct((1, 2, block_rows, new_rows.shape[2]), new_rows.dtype)
     row = jax.ShapeDtypeStruct((1, capacity + 1), jnp.int32)
     results = pl.pallas_call(
-        functools.partial(prepare_kernel, capacity),
-        out_shape=[jax.ShapeDtypeStruct((1, 2 * num_blk), jnp.int32)] + [row] * num_blk,
-        in_specs=[HBM] * 5,
-        out_specs=[SMEM] * (num_blk + 1),
-        scratch_shapes=[pltpu.SMEM(operand.shape, operand.dtype) for operand in operands]
+        functools.partial(prepare_kernel, capacity, to),
+        out_shape=[jax.ShapeDtypeStruct((1, 2 * num_blk), jnp.int32)]
+        + [row] * num_blk
+        + [block],
+        in_specs=[HBM] * 6,
+        out_specs=[SMEM] * (num_blk + 1) + [HBM],
+        scratch_shapes=[pltpu.SMEM(operand.shape, operand.dtype) for operand in operands[:5]]
         + [
+            pltpu.VMEM(new_rows.shape, new_rows.dtype),
             pltpu.SMEM((num_blk, capacity + 1), jnp.int32),
             pltpu.SMEM((num_blk,), jnp.int32),
             pltpu.SMEM((num_blk,), jnp.int32),
-            pltpu.SemaphoreType.DMA((5,)),
+            pltpu.SemaphoreType.DMA((6,)),
+            pltpu.SemaphoreType.DMA,
         ],
         compiler_params=pltpu.CompilerParams(vmem_limit_bytes=WHOLE_LIMIT),
     )(*operands)
-    return results[0], results[1:]
+    return results[0], results[1:-1], results[-1]
 
 
 def gather_kernel(plan, count, block_rows, direct, whole, count_ref, *refs):
@@ -394,9 +412,20 @@
     def shift(array, d):
         return lax.ppermute(array, "blk", [(i, (i + d) % num_blk) for i in range(num_blk)])
 
-    counts, asks = prepare(
-        prefix_slot, prefix_owner, prefix_len, write_slot, write_owner, capacity, num_blk
+    ahead = num_blk - shifts[0]
+    counts, asks, farthest = prepare(
+        prefix_slot,
+        prefix_owner,
+        prefix_len,
+        write_slot,
+        write_owner,
+        new_rows,
+        block_tok * kv_dev,
+        ahead,
+        capacity,
+        num_blk,
     )
+    farthest = shift(farthest, ahead)
     asked = {d: shift(asks[d], d) for d in shifts}
     rows = [asked[d] for d in shifts]
 
@@ -411,7 +440,7 @@
             pool_rows,
             new_rows,
             tuple(
-                (shifts.index(d), start, size, num_blk - d if first else None)
+                (shifts.index(d), start, size, num_blk - d if first and d != shifts[0] else None)
                 for d, start, size in plan
             ),
             after,
@@ -424,7 +453,7 @@
     loaded = load(plans[0], True)
     arrived = [send(plans[0], loaded)]
     local, new_pool = gather(
-        counts, [asks[0]], pool_rows, new_rows, ((0, 0, capacity, None),), loaded[:1], whole=True
+        counts, [asks[0]], pool_rows, new_rows, ((0, 0, capacity, None),), [loaded[0], farthest], whole=True
     )
     step = functools.partial(attend, counts, queries[0], kv_dev=kv_dev, block_tok=block_tok)
     state, _ = step([local], ((0, 0, capacity),), new_rows=new_rows)
@@ -454,7 +483,7 @@
                 write_slot,
                 [asked[num_blk - d] for d in shifts],
                 new_rows,
-                arrived[0],
+                [farthest, *arrived[0][1:]],
                 new_pool,
                 capacity,
             )

time: 123 us -> 121 us (0.984)
  waiting for transfers between devices: 59.8 us -> 54.7 us
  Pallas kernels: 42.1 us -> 44.6 us
    ppermute x12 -> x13, waiting for transfers between devices: 59.8 us -> 54.7 us  [shift(): lax.ppermute(array, 'blk', [(i, (i + d) % num_blk) for i in range(num_blk)])]
    pallas_call x4, Pallas kernels: 27.6 us -> 29.4 us  [attend(): pl.pallas_call(functools.partial(attend_kernel, spans, len(relay), len(af...]
    ppermute x12 -> x13, starting transfers between devices: 17.3 us -> 18.2 us  [shift(): lax.ppermute(array, 'blk', [(i, (i + d) % num_blk) for i in range(num_blk)])]
  transfers between devices with their start and end apart: 12 -> 13, of which waited for: 5 -> 4; matrix products, arithmetic and copies ran while one was open for 0% -> 0% of each run, Pallas kernels for 26% -> 30%
where the time goes in v1:
time: 121 us
  waiting for transfers between devices  54.7 us (45%)
  Pallas kernels  44.6 us (37%)
  starting transfers between devices  18.2 us (15%)
  between operations  1.67 us (1%)
  local copies, waits for them, and re-layouts  1.57 us (1%)
    ppermute x13, waiting for transfers between devices, shift(): lax.ppermute(array, 'blk', [(i, (i + d) % num_blk) for i in range(num_blk)])  54.7 us
    pallas_call x4, Pallas kernels, attend(): pl.pallas_call(functools.partial(attend_kernel, spans, len(relay), len(af...  29.4 us
    ppermute x13, starting transfers between devices, shift(): lax.ppermute(array, 'blk', [(i, (i + d) % num_blk) for i in range(num_blk)])  18.2 us
    pallas_call x3, Pallas kernels, gather(): pl.pallas_call(functools.partial(gather_kernel, plan, len(asked), pool.sh...  10.3 us
    pallas_call x1, Pallas kernels, prepare(): pl.pallas_call(functools.partial(prepare_kernel, capacity, to), out_shape...  2.44 us
  transfers between devices with their start and end apart: 13, of which 4 were waited for; matrix products, arithmetic and copies ran while one was open for 0% of the time, Pallas kernels for 30%

profile of v1, /device:TPU:14, one launch (start us, length us, event | category | flops | bytes accessed | tf_op | source)
XLA Modules:
  0.0 120.7 jit_solution(6732305329816046889)
XLA Ops:
  0.6 0.0 copy-start.1
  0.6 0.0 copy-start
  1.4 2.4 %shard_map.95 = (s32[1,8]{1,0:T(1,128)}, s32[1,9]{1,0:T(1,128)}, s32[1,9]{1,0:T(1,128)}, s32[1,9]{1,0:T(1,128)}, s32[1,9]{1,0:T(1,128)}, /*index=5*/bf16[1,2,256,128]{3,2,1,0:T(8,128)(2,1)}) custom-call(s32[1,32]{1,0:T(1,128)} %refs_0_.1, s32[1,32]{1,0:T(1,128)} %refs_1_.1, s32[1]{0:T(128)S(6)} %copy.18.refs_2_, s32[1,2]{1,0:T(1,128)} %slot_ref.1, ...), custom_call_target="tpu_custom_call" | custom-call | tf_op jit(solution)/shard_map/pallas_call | solution.py:85
  3.9 0.0 copy-start.3
  3.9 0.0 copy-start.12
  3.9 2.7 %collective-permute-start.3 = (bf16[1,2,256,128]{3,2,1,0:T(8,128)(2,1)}, bf16[1,2,256,128]{3,2,1,0:T(8,128)(2,1)S(1)}, u32[]{:S(2)}, u32[]{:S(2)}) collective-permute-start(bf16[1,2,256,128]{3,2,1,0:T(8,128)(2,1)} %get-tuple-element.37), channel_id=1, source_target_pairs={{0,8},{4,12},{8,0},{12,4},{1,9},{5,13},{9,1},{13,5},{2,10},{6,14},... | collective-permute-start | bytes 393224 | tf_op jit(solution)/shard_map/ppermute | solution.py:413
  6.6 0.3 collective-permute-start
  6.9 1.6 %collective-permute-start.1 = (s32[1,9]{1,0:T(1,128)}, s32[1,9]{1,0:T(1,128)S(1)}, u32[]{:S(2)}, u32[]{:S(2)}) collective-permute-start(s32[1,9]{1,0:T(1,128)} %get-tuple-element.34), channel_id=1, source_target_pairs={{0,4},{4,8},{8,12},{12,0},{1,5},{5,9},{9,13},{13,1},{2,6},{6,10},{... | collective-permute-start | bytes 116 | tf_op jit(solution)/shard_map/ppermute | solution.py:413
  8.5 0.4 collective-permute-start.2
  8.9 3.5 %collective-permute-done.refs_0_ = s32[1,9]{1,0:T(1,128)S(1)} collective-permute-done((s32[1,9]{1,0:T(1,128)}, s32[1,9]{1,0:T(1,128)S(1)}, u32[]{:S(2)}, u32[]{:S(2)}) %collective-permute-start) | collective-permute-done | bytes 68 | tf_op jit(solution)/shard_map/ppermute | solution.py:413
  12.4 0.0 collective-permute-done.1.refs_1_.refs_2_
  12.4 0.0 collective-permute-done.2.refs_2_.refs_1_
  12.4 0.0 copy-start.8
  12.4 0.5 copy-done.4
  12.9 0.0 copy-done.8
  12.9 3.2 %shard_map.96 = (bf16[3,2,256,128]{3,2,1,0:T(8,128)(2,1)}, bf16[4,2,256,128]{3,2,1,0:T(8,128)(2,1)}, bf16[4,2,256,128]{3,2,1,0:T(8,128)(2,1)}) custom-call(s32[1,8]{1,0:T(1,128)} %get-tuple-element.31.count_ref, s32[1,9]{1,0:T(1,128)} %copy-done.4, s32[1,9]{1,0:T(1,128)} %copy-done.6, s32[1,9]{1,0:T(1,128)} %copy-done.8, bf16[24,2,256,128]{3,2,1,0:T(8,128)(2,1)} %bitcast.5, ...), custom_call_target="tpu_custom_call" | custom-call | bytes 2883584 | tf_op jit(solution)/shard_map/pallas_call | solution.py:150
  16.1 1.1 collective-permute-start.5
  17.3 1.4 %collective-permute-start.6 = (bf16[4,2,256,128]{3,2,1,0:T(8,128)(2,1)}, bf16[4,2,256,128]{3,2,1,0:T(8,128)(2,1)S(1)}, u32[]{:S(2)}, u32[]{:S(2)}) collective-permute-start(bf16[4,2,256,128]{3,2,1,0:T(8,128)(2,1)} %get-tuple-element.41), channel_id=1, source_target_pairs={{0,4},{4,8},{8,12},{12,0},{1,5},{5,9},{9,13},{13,1},{2,6},{6,10},{... | collective-permute-start | bytes 1572872 | tf_op jit(solution)/shard_map/ppermute | solution.py:413
  18.6 4.7 %collective-permute-start.4 = (bf16[3,2,256,128]{3,2,1,0:T(8,128)(2,1)}, bf16[3,2,256,128]{3,2,1,0:T(8,128)(2,1)S(1)}, u32[]{:S(2)}, u32[]{:S(2)}) collective-permute-start(bf16[3,2,256,128]{3,2,1,0:T(8,128)(2,1)} %get-tuple-element.36.refs_3_), channel_id=1, source_target_pairs={{0,8},{4,12},{8,0},{12,4},{1,9},{5,13},{9,1},{13,5},{2,10},{6,14},... | collective-permute-start | bytes 1179656 | tf_op jit(solution)/shard_map/ppermute | solution.py:413
  23.3 0.0 collective-permute-done.3.refs_4_
  23.3 0.0 copy-done.1
  23.3 1.0 copy-done.2
  24.3 3.8 %shard_map.97 = (bf16[8,2,256,128]{3,2,1,0:T(8,128)(2,1)S(1)}, bf16[24,2,256,128]{3,2,1,0:T(8,128)(2,1)}) custom-call(s32[1,8]{1,0:T(1,128)S(1)} %copy-done.3, s32[1,9]{1,0:T(1,128)S(1)} %copy-done.12, bf16[24,2,256,128]{3,2,1,0:T(8,128)(2,1)S(1)} %bitcast.6, bf16[2,512,128]{2,1,0:T(8,128)(2,1)S(1)} %bitcast.10, bf16[3,2,256,128]{3,2,1,0:T(8,128)(2,1)S(1)} %copy-done.2, ...), custom_call_target="tpu_custom_call" | custom-call | bytes 8388608 | tf_op jit(solution)/shard_map/pallas_call | solution.py:150
  28.2 0.0 copy-done.13
  28.2 0.0 copy-start.5
  28.2 9.6 %shard_map.98 = (bf16[2,2048,128]{2,1,0:T(8,128)(2,1)S(1)}, f32[2,128,2048]{2,1,0:T(8,128)S(1)}, f32[2,8,2048]{2,1,0:T(8,128)S(1)}) custom-call(s32[1,8]{1,0:T(1,128)S(1)} %copy-done.3, bf16[256,16,128]{2,1,0:T(8,128)(2,1)S(1)} %bitcast.14, bf16[8,2,256,128]{3,2,1,0:T(8,128)(2,1)S(1)} %get-tuple-element.38.refs_0_, bf16[2,512,128]{2,1,0:T(8,128)(2,1)S(1)} %bitcast.11), custom_call_target="tpu_custom_call" | custom-call | flops 2684354560 | bytes 9699328 | tf_op jit(solution)/shard_map/pallas_call | solution.py:374
  37.9 3.3 %shard_map.99 = (bf16[3,2,256,128]{3,2,1,0:T(8,128)(2,1)S(1)}, bf16[3,2,256,128]{3,2,1,0:T(8,128)(2,1)S(1)}, bf16[3,2,256,128]{3,2,1,0:T(8,128)(2,1)S(1)}, bf16[...) custom-call(s32[1,8]{1,0:T(1,128)S(1)} %copy-done.3, ...), custom_call_target="tpu_custom_call" | custom-call | bytes 3932160 | tf_op jit(solution)/shard_map/pallas_call | solution.py:150
  41.2 0.1 collective-permute-start.10
  41.3 0.6 collective-permute-start.11
  41.8 34.4 %collective-permute-done.4.refs_0_ = bf16[3,2,256,128]{3,2,1,0:T(8,128)(2,1)S(1)} collective-permute-done((bf16[3,2,256,128]{3,2,1,0:T(8,128)(2,1)}, bf16[3,2,256,128]{3,2,1,0:T(8,128)(2,1)S(1)}, u32[]{:S(2)}, u32[]{:S(2)}) %collective-permute-start.4) | collective-permute-done | bytes 393248 | tf_op jit(solution)/shard_map/ppermute | solution.py:413
  76.2 0.0 collective-permute-start.12
  76.2 0.0 collective-permute-done.5.refs_1_.refs_5_
  76.2 0.0 collective-permute-done.6.refs_2_.refs_6_
  76.2 0.0 copy-start.10
  76.2 0.0 copy-start.11
  76.3 6.5 %shard_map.100 = (f32[2,128,2048]{2,1,0:T(8,128)S(1)}, f32[2,8,2048]{2,1,0:T(8,128)S(1)}, bf16[2,2,256,128]{3,2,1,0:T(8,128)(2,1)S(1)}, bf16[2,2,256,128]{3,2,1,0:T(8,128)(2,1)S(1)}, bf16[2,2,256,128]{3,2,1,0:T(8,128)(2,1)S(1)}) custom-call(s32[1,8]{1,0:T(1,128)S(1)} %copy-done.3, ...), custom_call_target="tpu_custom_call", output_to_operand_aliasing={{2}: (7, {}), {3}: (8, {}), {4}: (9, {})} | custom-call | flops 2415919104 | bytes 9568256 | tf_op jit(solution)/shard_map/pallas_call | solution.py:374
  82.8 3.3 %collective-permute-start.7 = (bf16[2,2,256,128]{3,2,1,0:T(8,128)(2,1)S(1)}, bf16[2,2,256,128]{3,2,1,0:T(8,128)(2,1)S(1)}, u32[]{:S(2)}, u32[]{:S(2)}) collective-permute-start(bf16[2,2,256,128]{3,2,1,0:T(8,128)(2,1)S(1)} %get-tuple-element.47), channel_id=1, source_target_pairs={{0,8},{4,12},{8,0},{12,4},{1,9},{5,13},{9,1},{13,5},{2,10},{6,14},... | collective-permute-start | bytes 786440 | tf_op jit(solution)/shard_map/ppermute | solution.py:413
  86.1 2.0 %collective-permute-start.8 = (bf16[2,2,256,128]{3,2,1,0:T(8,128)(2,1)S(1)}, bf16[2,2,256,128]{3,2,1,0:T(8,128)(2,1)S(1)}, u32[]{:S(2)}, u32[]{:S(2)}) collective-permute-start(bf16[2,2,256,128]{3,2,1,0:T(8,128)(2,1)S(1)} %get-tuple-element.48), channel_id=1, source_target_pairs={{0,12},{4,0},{8,4},{12,8},{1,13},{5,1},{9,5},{13,9},{2,14},{6,2},{... | collective-permute-start | bytes 786440 | tf_op jit(solution)/shard_map/ppermute | solution.py:413
  88.2 0.0 collective-permute-done.10.refs_0_
  88.2 0.0 collective-permute-start.9
  88.2 2.4 %shard_map.101 = (bf16[24,2,256,128]{3,2,1,0:T(8,128)(2,1)}, s32[1,1]{1,0:T(1,128)}) custom-call(s32[1,2]{1,0:T(1,128)S(1)} %copy-done.11, s32[1,2]{1,0:T(1,128)S(1)} %copy-done.10, s32[1,9]{1,0:T(1,128)S(1)} %copy-done.5, s32[1,9]{1,0:T(1,128)S(1)} %copy-done.9, s32[1,9]{1,0:T(1,128)S(1)} %copy-done.7, ...), custom_call_target="tpu_custom_call", output_to_operand_aliasing={{0}: (9, {})} | custom-call | bytes 1048576 | tf_op jit(solution)/shard_map/pallas_call | solution.py:189
  90.6 14.0 %collective-permute-done.11.refs_1_ = bf16[3,2,256,128]{3,2,1,0:T(8,128)(2,1)S(1)} collective-permute-done((bf16[3,2,256,128]{3,2,1,0:T(8,128)(2,1)S(1)}, bf16[3,2,256,128]{3,2,1,0:T(8,128)(2,1)S(1)}, u32[]{:S(2)}, u32[]{:S(2)}) %collective-permute-start.11) | collective-permute-done | bytes 393248 | tf_op jit(solution)/shard_map/ppermute | solution.py:413
  104.6 0.0 collective-permute-done.12.refs_2_
  104.6 7.4 %shard_map.102 = (f32[2,128,2048]{2,1,0:T(8,128)S(1)}, f32[2,8,2048]{2,1,0:T(8,128)S(1)}) custom-call(s32[1,8]{1,0:T(1,128)S(1)} %copy-done.3, bf16[2,2048,128]{2,1,0:T(8,128)(2,1)S(1)} %get-tuple-element.39.q_ref, bf16[3,2,256,128]{3,2,1,0:T(8,128)(2,1)S(1)} %collective-permute-done.10.refs_0_, ...), custom_call_target="tpu_custom_call" | custom-call | flops 2415919104 | bytes 9568256 | tf_op jit(solution)/shard_map/pallas_call | solution.py:374
  111.9 0.0 collective-permute-done.7.refs_0_
  111.9 2.9 %collective-permute-done.8.refs_1_ = bf16[2,2,256,128]{3,2,1,0:T(8,128)(2,1)S(1)} collective-permute-done((bf16[2,2,256,128]{3,2,1,0:T(8,128)(2,1)S(1)}, bf16[2,2,256,128]{3,2,1,0:T(8,128)(2,1)S(1)}, u32[]{:S(2)}, u32[]{:S(2)}) %collective-permute-start.8) | collective-permute-done | bytes 262176 | tf_op jit(solution)/shard_map/ppermute | solution.py:413
  114.8 0.0 collective-permute-done.9.refs_2_
  114.8 5.8 %shard_map.103 = bf16[256,16,128]{2,1,0:T(8,128)(2,1)} custom-call(s32[1,8]{1,0:T(1,128)S(1)} %copy-done.3, bf16[2,2048,128]{2,1,0:T(8,128)(2,1)S(1)} %get-tuple-element.39.q_ref, bf16[2,2,256,128]{3,2,1,0:T(8,128)(2,1)S(1)} %collective-permute-done.7.refs_0_, bf16[2,2,256,128]{3,2,1,0:T(8,128)(2,1)S(1)} %collective-permute-done.8.refs_1_, ...), custom_call_target="tpu_custom_call" | custom-call | flops 1610612736 | bytes 9175040 | tf_op jit(solution)/shard_map/pallas_call | solution.py:374
  (15 shorter events, 0.0 us)
Async XLA Ops:
  0.6 22.7 %copy-start.1 = (bf16[2,1,256,2,128]{4,3,2,1,0:T(2,128)(2,1)S(1)}, bf16[2,1,256,2,128]{4,3,2,1,0:T(2,128)(2,1)}, u32[]{:S(2)}) copy-start(bf16[2,1,256,2,128]{4,3,2,1,0:T(2,128)(2,1)} %param.9) | copy-start | bytes 786436
  0.6 22.7 %copy-start = (bf16[24,2,128,2,128]{4,3,2,1,0:T(2,128)(2,1)S(1)}, bf16[24,2,128,2,128]{4,3,2,1,0:T(2,128)(2,1)}, u32[]{:S(2)}) copy-start(bf16[24,2,128,2,128]{4,3,2,1,0:T(2,128)(2,1)} %param.10) | copy-start | bytes 9437188
  3.9 19.4 %copy-start.3 = (s32[1,8]{1,0:T(1,128)S(1)}, s32[1,8]{1,0:T(1,128)}, u32[]{:S(2)}) copy-start(s32[1,8]{1,0:T(1,128)} %get-tuple-element.31.count_ref) | copy-start | bytes 100
  3.9 19.4 %copy-start.12 = (s32[1,9]{1,0:T(1,128)S(1)}, s32[1,9]{1,0:T(1,128)}, u32[]{:S(2)}) copy-start(s32[1,9]{1,0:T(1,128)} %get-tuple-element.32.refs_0_) | copy-start | bytes 112
  3.9 19.4 %collective-permute-start.3 = (bf16[1,2,256,128]{3,2,1,0:T(8,128)(2,1)}, bf16[1,2,256,128]{3,2,1,0:T(8,128)(2,1)S(1)}, u32[]{:S(2)}, u32[]{:S(2)}) collective-permute-start(bf16[1,2,256,128]{3,2,1,0:T(8,128)(2,1)} %get-tuple-element.37), channel_id=1, source_target_pairs={{0,8},{4,12},{8,0},{12,4},{1,9},{5,13},{9,1},{13,5},{2,10},{6,14},... | collective-permute-start | bytes 393224 | tf_op jit(solution)/shard_map/ppermute | solution.py:413
  6.6 5.8 %collective-permute-start = (s32[1,9]{1,0:T(1,128)}, s32[1,9]{1,0:T(1,128)S(1)}, u32[]{:S(2)}, u32[]{:S(2)}) collective-permute-start(s32[1,9]{1,0:T(1,128)} %get-tuple-element.33), channel_id=1, source_target_pairs={{0,8},{4,12},{8,0},{12,4},{1,9},{5,13},{9,1},{13,5},{2,10},{6,14},... | collective-permute-start | bytes 116 | tf_op jit(solution)/shard_map/ppermute | solution.py:413
  6.9 5.5 %collective-permute-start.1 = (s32[1,9]{1,0:T(1,128)}, s32[1,9]{1,0:T(1,128)S(1)}, u32[]{:S(2)}, u32[]{:S(2)}) collective-permute-start(s32[1,9]{1,0:T(1,128)} %get-tuple-element.34), channel_id=1, source_target_pairs={{0,4},{4,8},{8,12},{12,0},{1,5},{5,9},{9,13},{13,1},{2,6},{6,10},{... | collective-permute-start | bytes 116 | tf_op jit(solution)/shard_map/ppermute | solution.py:413
  8.5 3.9 %collective-permute-start.2 = (s32[1,9]{1,0:T(1,128)}, s32[1,9]{1,0:T(1,128)S(1)}, u32[]{:S(2)}, u32[]{:S(2)}) collective-permute-start(s32[1,9]{1,0:T(1,128)} %get-tuple-element.35), channel_id=1, source_target_pairs={{0,12},{4,0},{8,4},{12,8},{1,13},{5,1},{9,5},{13,9},{2,14},{6,2},{... | collective-permute-start | bytes 116 | tf_op jit(solution)/shard_map/ppermute | solution.py:413
  12.4 0.5 copy-start.4
  12.4 0.5 copy-start.6
  12.4 0.5 copy-start.8
  16.1 60.1 %collective-permute-start.5 = (bf16[4,2,256,128]{3,2,1,0:T(8,128)(2,1)}, bf16[4,2,256,128]{3,2,1,0:T(8,128)(2,1)S(1)}, u32[]{:S(2)}, u32[]{:S(2)}) collective-permute-start(bf16[4,2,256,128]{3,2,1,0:T(8,128)(2,1)} %get-tuple-element.40), channel_id=1, source_target_pairs={{0,12},{4,0},{8,4},{12,8},{1,13},{5,1},{9,5},{13,9},{2,14},{6,2},{... | collective-permute-start | bytes 1572872 | tf_op jit(solution)/shard_map/ppermute | solution.py:413
  17.3 59.0 %collective-permute-start.6 = (bf16[4,2,256,128]{3,2,1,0:T(8,128)(2,1)}, bf16[4,2,256,128]{3,2,1,0:T(8,128)(2,1)S(1)}, u32[]{:S(2)}, u32[]{:S(2)}) collective-permute-start(bf16[4,2,256,128]{3,2,1,0:T(8,128)(2,1)} %get-tuple-element.41), channel_id=1, source_target_pairs={{0,4},{4,8},{8,12},{12,0},{1,5},{5,9},{9,13},{13,1},{2,6},{6,10},{... | collective-permute-start | bytes 1572872 | tf_op jit(solution)/shard_map/ppermute | solution.py:413
  18.6 57.6 %collective-permute-start.4 = (bf16[3,2,256,128]{3,2,1,0:T(8,128)(2,1)}, bf16[3,2,256,128]{3,2,1,0:T(8,128)(2,1)S(1)}, u32[]{:S(2)}, u32[]{:S(2)}) collective-permute-start(bf16[3,2,256,128]{3,2,1,0:T(8,128)(2,1)} %get-tuple-element.36.refs_3_), channel_id=1, source_target_pairs={{0,8},{4,12},{8,0},{12,4},{1,9},{5,13},{9,1},{13,5},{2,10},{6,14},... | collective-permute-start | bytes 1179656 | tf_op jit(solution)/shard_map/ppermute | solution.py:413
  23.3 1.0 copy-start.2
  24.3 3.9 %copy-start.13 = (bf16[1,256,16,128]{3,2,1,0:T(8,128)(2,1)S(1)}, bf16[1,256,16,128]{3,2,1,0:T(8,128)(2,1)}, u32[]{:S(2)}) copy-start(bf16[1,256,16,128]{3,2,1,0:T(8,128)(2,1)} %param.8) | copy-start | bytes 3145732
  28.2 9.7 %copy-start.5 = (s32[1,9]{1,0:T(1,128)S(1)}, s32[1,9]{1,0:T(1,128)}, u32[]{:S(2)}) copy-start(s32[1,9]{1,0:T(1,128)} %copy-done.4) | copy-start | bytes 112
  28.2 9.7 %copy-start.7 = (s32[1,9]{1,0:T(1,128)S(1)}, s32[1,9]{1,0:T(1,128)}, u32[]{:S(2)}) copy-start(s32[1,9]{1,0:T(1,128)} %copy-done.6) | copy-start | bytes 112
  28.2 9.7 %copy-start.9 = (s32[1,9]{1,0:T(1,128)S(1)}, s32[1,9]{1,0:T(1,128)}, u32[]{:S(2)}) copy-start(s32[1,9]{1,0:T(1,128)} %copy-done.8) | copy-start | bytes 112
  41.2 46.9 %collective-permute-start.10 = (bf16[3,2,256,128]{3,2,1,0:T(8,128)(2,1)S(1)}, bf16[3,2,256,128]{3,2,1,0:T(8,128)(2,1)S(1)}, u32[]{:S(2)}, u32[]{:S(2)}) collective-permute-start(bf16[3,2,256,128]{3,2,1,0:T(8,128)(2,1)S(1)} %get-tuple-element.50), channel_id=1, source_target_pairs={{0,8},{4,12},{8,0},{12,4},{1,9},{5,13},{9,1},{13,5},{2,10},{6,14},... | collective-permute-start | bytes 1179656 | tf_op jit(solution)/shard_map/ppermute | solution.py:413
  41.3 63.3 %collective-permute-start.11 = (bf16[3,2,256,128]{3,2,1,0:T(8,128)(2,1)S(1)}, bf16[3,2,256,128]{3,2,1,0:T(8,128)(2,1)S(1)}, u32[]{:S(2)}, u32[]{:S(2)}) collective-permute-start(bf16[3,2,256,128]{3,2,1,0:T(8,128)(2,1)S(1)} %get-tuple-element.51), channel_id=1, source_target_pairs={{0,12},{4,0},{8,4},{12,8},{1,13},{5,1},{9,5},{13,9},{2,14},{6,2},{... | collective-permute-start | bytes 1179656 | tf_op jit(solution)/shard_map/ppermute | solution.py:413
  76.2 28.3 %collective-permute-start.12 = (bf16[3,2,256,128]{3,2,1,0:T(8,128)(2,1)S(1)}, bf16[3,2,256,128]{3,2,1,0:T(8,128)(2,1)S(1)}, u32[]{:S(2)}, u32[]{:S(2)}) collective-permute-start(bf16[3,2,256,128]{3,2,1,0:T(8,128)(2,1)S(1)} %get-tuple-element.52), channel_id=1, source_target_pairs={{0,4},{4,8},{8,12},{12,0},{1,5},{5,9},{9,13},{13,1},{2,6},{6,10},{... | collective-permute-start | bytes 1179656 | tf_op jit(solution)/shard_map/ppermute | solution.py:413
  76.2 11.9 %copy-start.10 = (s32[1,2]{1,0:T(1,128)S(1)}, s32[1,2]{1,0:T(1,128)}, u32[]{:S(2)}) copy-start(s32[1,2]{1,0:T(1,128)} %slot_ref.1) | copy-start | bytes 28
  76.2 11.9 %copy-start.11 = (s32[1,2]{1,0:T(1,128)S(1)}, s32[1,2]{1,0:T(1,128)}, u32[]{:S(2)}) copy-start(s32[1,2]{1,0:T(1,128)} %owner_ref.1) | copy-start | bytes 28
  82.8 29.1 %collective-permute-start.7 = (bf16[2,2,256,128]{3,2,1,0:T(8,128)(2,1)S(1)}, bf16[2,2,256,128]{3,2,1,0:T(8,128)(2,1)S(1)}, u32[]{:S(2)}, u32[]{:S(2)}) collective-permute-start(bf16[2,2,256,128]{3,2,1,0:T(8,128)(2,1)S(1)} %get-tuple-element.47), channel_id=1, source_target_pairs={{0,8},{4,12},{8,0},{12,4},{1,9},{5,13},{9,1},{13,5},{2,10},{6,14},... | collective-permute-start | bytes 786440 | tf_op jit(solution)/shard_map/ppermute | solution.py:413
  86.1 28.7 %collective-permute-start.8 = (bf16[2,2,256,128]{3,2,1,0:T(8,128)(2,1)S(1)}, bf16[2,2,256,128]{3,2,1,0:T(8,128)(2,1)S(1)}, u32[]{:S(2)}, u32[]{:S(2)}) collective-permute-start(bf16[2,2,256,128]{3,2,1,0:T(8,128)(2,1)S(1)} %get-tuple-element.48), channel_id=1, source_target_pairs={{0,12},{4,0},{8,4},{12,8},{1,13},{5,1},{9,5},{13,9},{2,14},{6,2},{... | collective-permute-start | bytes 786440 | tf_op jit(solution)/shard_map/ppermute | solution.py:413
  88.2 26.7 %collective-permute-start.9 = (bf16[2,2,256,128]{3,2,1,0:T(8,128)(2,1)S(1)}, bf16[2,2,256,128]{3,2,1,0:T(8,128)(2,1)S(1)}, u32[]{:S(2)}, u32[]{:S(2)}) collective-permute-start(bf16[2,2,256,128]{3,2,1,0:T(8,128)(2,1)S(1)} %get-tuple-element.49), channel_id=1, source_target_pairs={{0,4},{4,8},{8,12},{12,0},{1,5},{5,9},{9,13},{13,1},{2,6},{6,10},{... | collective-permute-start | bytes 786440 | tf_op jit(solution)/shard_map/ppermute | solution.py:413

commit v2 on v1

--- a/solution.py
+++ b/solution.py
@@ -339,7 +339,11 @@
             return worst
 
         worst = lax.fori_loop(
-            0, q_rows.shape[1] // rows, sub, jnp.full((1, rows), -jnp.inf, jnp.float32)
+            0,
+            q_rows.shape[1] // rows,
+            sub,
+            jnp.full((1, rows), -jnp.inf, jnp.float32),
+            unroll=not safe,
         )
         if not first and not safe:
 

time: 121 us -> 121 us (level)
  Pallas kernels: 44.6 us -> 41.1 us
  waiting for transfers between devices: 54.7 us -> 56.1 us
    pallas_call x4, Pallas kernels: 29.4 us -> 26.1 us  [attend(): pl.pallas_call(functools.partial(attend_kernel, spans, len(relay), len(af...]
    ppermute x13, waiting for transfers between devices: 54.7 us -> 56.1 us  [shift(): lax.ppermute(array, 'blk', [(i, (i + d) % num_blk) for i in range(num_blk)])]
  transfers between devices with their start and end apart: 13 -> 13, of which waited for: 4 -> 4; matrix products, arithmetic and copies ran while one was open for 0% -> 0% of each run, Pallas kernels for 30% -> 28%
where the time goes in v2:
time: 121 us; the launch traced here: 120 us
  waiting for transfers between devices  56.1 us (46%)
  Pallas kernels  41.1 us (34%)
  starting transfers between devices  19.2 us (16%)
  between operations  1.67 us (1%)
  local copies, waits for them, and re-layouts  1.57 us (1%)
    ppermute x13, waiting for transfers between devices, shift(): lax.ppermute(array, 'blk', [(i, (i + d) % num_blk) for i in range(num_blk)])  56.1 us
    pallas_call x4, Pallas kernels, attend(): pl.pallas_call(functools.partial(attend_kernel, spans, len(relay), len(af...  26.1 us
    ppermute x13, starting transfers between devices, shift(): lax.ppermute(array, 'blk', [(i, (i + d) % num_blk) for i in range(num_blk)])  19.2 us
    pallas_call x3, Pallas kernels, gather(): pl.pallas_call(functools.partial(gather_kernel, plan, len(asked), pool.sh...  10.1 us
    pallas_call x1, Pallas kernels, prepare(): pl.pallas_call(functools.partial(prepare_kernel, capacity, to), out_shape...  2.44 us
  transfers between devices with their start and end apart: 13, of which 4 were waited for; matrix products, arithmetic and copies ran while one was open for 0% of the time, Pallas kernels for 28%

profile of v2, /device:TPU:14, one launch (start us, length us, event | category | flops | bytes accessed | tf_op | source)
XLA Modules:
  0.0 119.5 jit_solution(16831229374882189676)
XLA Ops:
  0.6 0.0 copy-start.1
  0.6 0.0 copy-start
  1.4 2.4 %shard_map.95 = (s32[1,8]{1,0:T(1,128)}, s32[1,9]{1,0:T(1,128)}, s32[1,9]{1,0:T(1,128)}, s32[1,9]{1,0:T(1,128)}, s32[1,9]{1,0:T(1,128)}, /*index=5*/bf16[1,2,256,128]{3,2,1,0:T(8,128)(2,1)}) custom-call(s32[1,32]{1,0:T(1,128)} %refs_0_.1, s32[1,32]{1,0:T(1,128)} %refs_1_.1, s32[1]{0:T(128)S(6)} %copy.18.refs_2_, s32[1,2]{1,0:T(1,128)} %slot_ref.1, ...), custom_call_target="tpu_custom_call" | custom-call | tf_op jit(solution)/shard_map/pallas_call | solution.py:85
  3.9 0.0 copy-start.3
  3.9 0.0 copy-start.12
  3.9 2.7 %collective-permute-start.3 = (bf16[1,2,256,128]{3,2,1,0:T(8,128)(2,1)}, bf16[1,2,256,128]{3,2,1,0:T(8,128)(2,1)S(1)}, u32[]{:S(2)}, u32[]{:S(2)}) collective-permute-start(bf16[1,2,256,128]{3,2,1,0:T(8,128)(2,1)} %get-tuple-element.37), channel_id=1, source_target_pairs={{0,8},{4,12},{8,0},{12,4},{1,9},{5,13},{9,1},{13,5},{2,10},{6,14},... | collective-permute-start | bytes 393224 | tf_op jit(solution)/shard_map/ppermute | solution.py:417
  6.6 0.3 collective-permute-start
  6.9 1.6 %collective-permute-start.1 = (s32[1,9]{1,0:T(1,128)}, s32[1,9]{1,0:T(1,128)S(1)}, u32[]{:S(2)}, u32[]{:S(2)}) collective-permute-start(s32[1,9]{1,0:T(1,128)} %get-tuple-element.34), channel_id=1, source_target_pairs={{0,4},{4,8},{8,12},{12,0},{1,5},{5,9},{9,13},{13,1},{2,6},{6,10},{... | collective-permute-start | bytes 116 | tf_op jit(solution)/shard_map/ppermute | solution.py:417
  8.5 0.4 collective-permute-start.2
  8.9 3.5 %collective-permute-done.refs_0_ = s32[1,9]{1,0:T(1,128)S(1)} collective-permute-done((s32[1,9]{1,0:T(1,128)}, s32[1,9]{1,0:T(1,128)S(1)}, u32[]{:S(2)}, u32[]{:S(2)}) %collective-permute-start) | collective-permute-done | bytes 68 | tf_op jit(solution)/shard_map/ppermute | solution.py:417
  12.4 0.0 collective-permute-done.1.refs_1_.refs_2_
  12.4 0.0 collective-permute-done.2.refs_2_.refs_1_
  12.4 0.0 copy-start.8
  12.4 0.5 copy-done.4
  12.9 0.0 copy-done.8
  12.9 3.0 %shard_map.96 = (bf16[3,2,256,128]{3,2,1,0:T(8,128)(2,1)}, bf16[4,2,256,128]{3,2,1,0:T(8,128)(2,1)}, bf16[4,2,256,128]{3,2,1,0:T(8,128)(2,1)}) custom-call(s32[1,8]{1,0:T(1,128)} %get-tuple-element.31.count_ref, s32[1,9]{1,0:T(1,128)} %copy-done.4, s32[1,9]{1,0:T(1,128)} %copy-done.6, s32[1,9]{1,0:T(1,128)} %copy-done.8, bf16[24,2,256,128]{3,2,1,0:T(8,128)(2,1)} %bitcast.5, ...), custom_call_target="tpu_custom_call" | custom-call | bytes 2883584 | tf_op jit(solution)/shard_map/pallas_call | solution.py:150
  15.9 1.3 %collective-permute-start.5 = (bf16[4,2,256,128]{3,2,1,0:T(8,128)(2,1)}, bf16[4,2,256,128]{3,2,1,0:T(8,128)(2,1)S(1)}, u32[]{:S(2)}, u32[]{:S(2)}) collective-permute-start(bf16[4,2,256,128]{3,2,1,0:T(8,128)(2,1)} %get-tuple-element.40), channel_id=1, source_target_pairs={{0,12},{4,0},{8,4},{12,8},{1,13},{5,1},{9,5},{13,9},{2,14},{6,2},{... | collective-permute-start | bytes 1572872 | tf_op jit(solution)/shard_map/ppermute | solution.py:417
  17.3 1.1 collective-permute-start.6
  18.3 4.8 %collective-permute-start.4 = (bf16[3,2,256,128]{3,2,1,0:T(8,128)(2,1)}, bf16[3,2,256,128]{3,2,1,0:T(8,128)(2,1)S(1)}, u32[]{:S(2)}, u32[]{:S(2)}) collective-permute-start(bf16[3,2,256,128]{3,2,1,0:T(8,128)(2,1)} %get-tuple-element.36.refs_3_), channel_id=1, source_target_pairs={{0,8},{4,12},{8,0},{12,4},{1,9},{5,13},{9,1},{13,5},{2,10},{6,14},... | collective-permute-start | bytes 1179656 | tf_op jit(solution)/shard_map/ppermute | solution.py:417
  23.1 0.0 collective-permute-done.3.refs_4_
  23.1 0.0 copy-done.3
  23.1 0.0 copy-done.12
  23.1 0.0 copy-start.2
  23.1 1.0 copy-done.2
  24.1 3.8 %shard_map.97 = (bf16[8,2,256,128]{3,2,1,0:T(8,128)(2,1)S(1)}, bf16[24,2,256,128]{3,2,1,0:T(8,128)(2,1)}) custom-call(s32[1,8]{1,0:T(1,128)S(1)} %copy-done.3, s32[1,9]{1,0:T(1,128)S(1)} %copy-done.12, bf16[24,2,256,128]{3,2,1,0:T(8,128)(2,1)S(1)} %bitcast.6, bf16[2,512,128]{2,1,0:T(8,128)(2,1)S(1)} %bitcast.10, bf16[3,2,256,128]{3,2,1,0:T(8,128)(2,1)S(1)} %copy-done.2, ...), custom_call_target="tpu_custom_call" | custom-call | bytes 8388608 | tf_op jit(solution)/shard_map/pallas_call | solution.py:150
  28.0 9.2 %shard_map.98 = (bf16[2,2048,128]{2,1,0:T(8,128)(2,1)S(1)}, f32[2,128,2048]{2,1,0:T(8,128)S(1)}, f32[2,8,2048]{2,1,0:T(8,128)S(1)}) custom-call(s32[1,8]{1,0:T(1,128)S(1)} %copy-done.3, bf16[256,16,128]{2,1,0:T(8,128)(2,1)S(1)} %bitcast.14, bf16[8,2,256,128]{3,2,1,0:T(8,128)(2,1)S(1)} %get-tuple-element.38.refs_0_, bf16[2,512,128]{2,1,0:T(8,128)(2,1)S(1)} %bitcast.11), custom_call_target="tpu_custom_call" | custom-call | flops 2684354560 | bytes 9699328 | tf_op jit(solution)/shard_map/pallas_call | solution.py:378
  37.2 3.3 %shard_map.99 = (bf16[3,2,256,128]{3,2,1,0:T(8,128)(2,1)S(1)}, bf16[3,2,256,128]{3,2,1,0:T(8,128)(2,1)S(1)}, bf16[3,2,256,128]{3,2,1,0:T(8,128)(2,1)S(1)}, bf16[...) custom-call(s32[1,8]{1,0:T(1,128)S(1)} %copy-done.3, ...), custom_call_target="tpu_custom_call" | custom-call | bytes 3932160 | tf_op jit(solution)/shard_map/pallas_call | solution.py:150
  40.5 0.3 collective-permute-start.10
  40.8 0.8 collective-permute-start.11
  41.6 34.3 %collective-permute-done.4.refs_0_ = bf16[3,2,256,128]{3,2,1,0:T(8,128)(2,1)S(1)} collective-permute-done((bf16[3,2,256,128]{3,2,1,0:T(8,128)(2,1)}, bf16[3,2,256,128]{3,2,1,0:T(8,128)(2,1)S(1)}, u32[]{:S(2)}, u32[]{:S(2)}) %collective-permute-start.4) | collective-permute-done | bytes 393248 | tf_op jit(solution)/shard_map/ppermute | solution.py:417
  75.9 0.0 collective-permute-start.12
  75.9 0.0 collective-permute-done.5.refs_1_.refs_5_
  75.9 0.0 collective-permute-done.6.refs_2_.refs_6_
  76.0 0.0 copy-start.10
  76.0 0.0 copy-start.11
  76.0 5.9 %shard_map.100 = (f32[2,128,2048]{2,1,0:T(8,128)S(1)}, f32[2,8,2048]{2,1,0:T(8,128)S(1)}, bf16[2,2,256,128]{3,2,1,0:T(8,128)(2,1)S(1)}, bf16[2,2,256,128]{3,2,1,0:T(8,128)(2,1)S(1)}, bf16[2,2,256,128]{3,2,1,0:T(8,128)(2,1)S(1)}) custom-call(s32[1,8]{1,0:T(1,128)S(1)} %copy-done.3, ...), custom_call_target="tpu_custom_call", output_to_operand_aliasing={{2}: (7, {}), {3}: (8, {}), {4}: (9, {})} | custom-call | flops 2415919104 | bytes 9568256 | tf_op jit(solution)/shard_map/pallas_call | solution.py:378
  81.9 3.7 %collective-permute-start.7 = (bf16[2,2,256,128]{3,2,1,0:T(8,128)(2,1)S(1)}, bf16[2,2,256,128]{3,2,1,0:T(8,128)(2,1)S(1)}, u32[]{:S(2)}, u32[]{:S(2)}) collective-permute-start(bf16[2,2,256,128]{3,2,1,0:T(8,128)(2,1)S(1)} %get-tuple-element.47), channel_id=1, source_target_pairs={{0,8},{4,12},{8,0},{12,4},{1,9},{5,13},{9,1},{13,5},{2,10},{6,14},... | collective-permute-start | bytes 786440 | tf_op jit(solution)/shard_map/ppermute | solution.py:417
  85.7 2.1 %collective-permute-start.8 = (bf16[2,2,256,128]{3,2,1,0:T(8,128)(2,1)S(1)}, bf16[2,2,256,128]{3,2,1,0:T(8,128)(2,1)S(1)}, u32[]{:S(2)}, u32[]{:S(2)}) collective-permute-start(bf16[2,2,256,128]{3,2,1,0:T(8,128)(2,1)S(1)} %get-tuple-element.48), channel_id=1, source_target_pairs={{0,12},{4,0},{8,4},{12,8},{1,13},{5,1},{9,5},{13,9},{2,14},{6,2},{... | collective-permute-start | bytes 786440 | tf_op jit(solution)/shard_map/ppermute | solution.py:417
  87.8 0.0 collective-permute-done.10.refs_0_
  87.8 0.0 collective-permute-start.9
  87.8 2.4 %shard_map.101 = (bf16[24,2,256,128]{3,2,1,0:T(8,128)(2,1)}, s32[1,1]{1,0:T(1,128)}) custom-call(s32[1,2]{1,0:T(1,128)S(1)} %copy-done.11, s32[1,2]{1,0:T(1,128)S(1)} %copy-done.10, s32[1,9]{1,0:T(1,128)S(1)} %copy-done.5, s32[1,9]{1,0:T(1,128)S(1)} %copy-done.9, s32[1,9]{1,0:T(1,128)S(1)} %copy-done.7, ...), custom_call_target="tpu_custom_call", output_to_operand_aliasing={{0}: (9, {})} | custom-call | bytes 1048576 | tf_op jit(solution)/shard_map/pallas_call | solution.py:189
  90.2 14.1 %collective-permute-done.11.refs_1_ = bf16[3,2,256,128]{3,2,1,0:T(8,128)(2,1)S(1)} collective-permute-done((bf16[3,2,256,128]{3,2,1,0:T(8,128)(2,1)S(1)}, bf16[3,2,256,128]{3,2,1,0:T(8,128)(2,1)S(1)}, u32[]{:S(2)}, u32[]{:S(2)}) %collective-permute-start.11) | collective-permute-done | bytes 393248 | tf_op jit(solution)/shard_map/ppermute | solution.py:417
  104.3 0.0 collective-permute-done.12.refs_2_
  104.3 6.0 %shard_map.102 = (f32[2,128,2048]{2,1,0:T(8,128)S(1)}, f32[2,8,2048]{2,1,0:T(8,128)S(1)}) custom-call(s32[1,8]{1,0:T(1,128)S(1)} %copy-done.3, bf16[2,2048,128]{2,1,0:T(8,128)(2,1)S(1)} %get-tuple-element.39.q_ref, bf16[3,2,256,128]{3,2,1,0:T(8,128)(2,1)S(1)} %collective-permute-done.10.refs_0_, ...), custom_call_target="tpu_custom_call" | custom-call | flops 2415919104 | bytes 9568256 | tf_op jit(solution)/shard_map/pallas_call | solution.py:378
  110.3 0.0 collective-permute-done.7.refs_0_
  110.3 4.2 %collective-permute-done.8.refs_1_ = bf16[2,2,256,128]{3,2,1,0:T(8,128)(2,1)S(1)} collective-permute-done((bf16[2,2,256,128]{3,2,1,0:T(8,128)(2,1)S(1)}, bf16[2,2,256,128]{3,2,1,0:T(8,128)(2,1)S(1)}, u32[]{:S(2)}, u32[]{:S(2)}) %collective-permute-start.8) | collective-permute-done | bytes 262176 | tf_op jit(solution)/shard_map/ppermute | solution.py:417
  114.6 0.0 collective-permute-done.9.refs_2_
  114.6 5.0 %shard_map.103 = bf16[256,16,128]{2,1,0:T(8,128)(2,1)} custom-call(s32[1,8]{1,0:T(1,128)S(1)} %copy-done.3, bf16[2,2048,128]{2,1,0:T(8,128)(2,1)S(1)} %get-tuple-element.39.q_ref, bf16[2,2,256,128]{3,2,1,0:T(8,128)(2,1)S(1)} %collective-permute-done.7.refs_0_, bf16[2,2,256,128]{3,2,1,0:T(8,128)(2,1)S(1)} %collective-permute-done.8.refs_1_, ...), custom_call_target="tpu_custom_call" | custom-call | flops 1610612736 | bytes 9175040 | tf_op jit(solution)/shard_map/pallas_call | solution.py:378
  (15 shorter events, 0.0 us)
Async XLA Ops:
  0.6 22.5 %copy-start.1 = (bf16[2,1,256,2,128]{4,3,2,1,0:T(2,128)(2,1)S(1)}, bf16[2,1,256,2,128]{4,3,2,1,0:T(2,128)(2,1)}, u32[]{:S(2)}) copy-start(bf16[2,1,256,2,128]{4,3,2,1,0:T(2,128)(2,1)} %param.9) | copy-start | bytes 786436
  0.6 22.5 %copy-start = (bf16[24,2,128,2,128]{4,3,2,1,0:T(2,128)(2,1)S(1)}, bf16[24,2,128,2,128]{4,3,2,1,0:T(2,128)(2,1)}, u32[]{:S(2)}) copy-start(bf16[24,2,128,2,128]{4,3,2,1,0:T(2,128)(2,1)} %param.10) | copy-start | bytes 9437188
  3.9 19.2 %copy-start.3 = (s32[1,8]{1,0:T(1,128)S(1)}, s32[1,8]{1,0:T(1,128)}, u32[]{:S(2)}) copy-start(s32[1,8]{1,0:T(1,128)} %get-tuple-element.31.count_ref) | copy-start | bytes 100
  3.9 19.2 %copy-start.12 = (s32[1,9]{1,0:T(1,128)S(1)}, s32[1,9]{1,0:T(1,128)}, u32[]{:S(2)}) copy-start(s32[1,9]{1,0:T(1,128)} %get-tuple-element.32.refs_0_) | copy-start | bytes 112
  3.9 19.2 %collective-permute-start.3 = (bf16[1,2,256,128]{3,2,1,0:T(8,128)(2,1)}, bf16[1,2,256,128]{3,2,1,0:T(8,128)(2,1)S(1)}, u32[]{:S(2)}, u32[]{:S(2)}) collective-permute-start(bf16[1,2,256,128]{3,2,1,0:T(8,128)(2,1)} %get-tuple-element.37), channel_id=1, source_target_pairs={{0,8},{4,12},{8,0},{12,4},{1,9},{5,13},{9,1},{13,5},{2,10},{6,14},... | collective-permute-start | bytes 393224 | tf_op jit(solution)/shard_map/ppermute | solution.py:417
  6.6 5.8 %collective-permute-start = (s32[1,9]{1,0:T(1,128)}, s32[1,9]{1,0:T(1,128)S(1)}, u32[]{:S(2)}, u32[]{:S(2)}) collective-permute-start(s32[1,9]{1,0:T(1,128)} %get-tuple-element.33), channel_id=1, source_target_pairs={{0,8},{4,12},{8,0},{12,4},{1,9},{5,13},{9,1},{13,5},{2,10},{6,14},... | collective-permute-start | bytes 116 | tf_op jit(solution)/shard_map/ppermute | solution.py:417
  6.9 5.5 %collective-permute-start.1 = (s32[1,9]{1,0:T(1,128)}, s32[1,9]{1,0:T(1,128)S(1)}, u32[]{:S(2)}, u32[]{:S(2)}) collective-permute-start(s32[1,9]{1,0:T(1,128)} %get-tuple-element.34), channel_id=1, source_target_pairs={{0,4},{4,8},{8,12},{12,0},{1,5},{5,9},{9,13},{13,1},{2,6},{6,10},{... | collective-permute-start | bytes 116 | tf_op jit(solution)/shard_map/ppermute | solution.py:417
  8.5 3.9 %collective-permute-start.2 = (s32[1,9]{1,0:T(1,128)}, s32[1,9]{1,0:T(1,128)S(1)}, u32[]{:S(2)}, u32[]{:S(2)}) collective-permute-start(s32[1,9]{1,0:T(1,128)} %get-tuple-element.35), channel_id=1, source_target_pairs={{0,12},{4,0},{8,4},{12,8},{1,13},{5,1},{9,5},{13,9},{2,14},{6,2},{... | collective-permute-start | bytes 116 | tf_op jit(solution)/shard_map/ppermute | solution.py:417
  12.4 0.5 copy-start.4
  12.4 0.5 copy-start.6
  12.4 0.5 copy-start.8
  15.9 60.0 %collective-permute-start.5 = (bf16[4,2,256,128]{3,2,1,0:T(8,128)(2,1)}, bf16[4,2,256,128]{3,2,1,0:T(8,128)(2,1)S(1)}, u32[]{:S(2)}, u32[]{:S(2)}) collective-permute-start(bf16[4,2,256,128]{3,2,1,0:T(8,128)(2,1)} %get-tuple-element.40), channel_id=1, source_target_pairs={{0,12},{4,0},{8,4},{12,8},{1,13},{5,1},{9,5},{13,9},{2,14},{6,2},{... | collective-permute-start | bytes 1572872 | tf_op jit(solution)/shard_map/ppermute | solution.py:417
  17.3 58.7 %collective-permute-start.6 = (bf16[4,2,256,128]{3,2,1,0:T(8,128)(2,1)}, bf16[4,2,256,128]{3,2,1,0:T(8,128)(2,1)S(1)}, u32[]{:S(2)}, u32[]{:S(2)}) collective-permute-start(bf16[4,2,256,128]{3,2,1,0:T(8,128)(2,1)} %get-tuple-element.41), channel_id=1, source_target_pairs={{0,4},{4,8},{8,12},{12,0},{1,5},{5,9},{9,13},{13,1},{2,6},{6,10},{... | collective-permute-start | bytes 1572872 | tf_op jit(solution)/shard_map/ppermute | solution.py:417
  18.3 57.6 %collective-permute-start.4 = (bf16[3,2,256,128]{3,2,1,0:T(8,128)(2,1)}, bf16[3,2,256,128]{3,2,1,0:T(8,128)(2,1)S(1)}, u32[]{:S(2)}, u32[]{:S(2)}) collective-permute-start(bf16[3,2,256,128]{3,2,1,0:T(8,128)(2,1)} %get-tuple-element.36.refs_3_), channel_id=1, source_target_pairs={{0,8},{4,12},{8,0},{12,4},{1,9},{5,13},{9,1},{13,5},{2,10},{6,14},... | collective-permute-start | bytes 1179656 | tf_op jit(solution)/shard_map/ppermute | solution.py:417
  23.1 1.0 copy-start.2
  24.1 3.9 %copy-start.13 = (bf16[1,256,16,128]{3,2,1,0:T(8,128)(2,1)S(1)}, bf16[1,256,16,128]{3,2,1,0:T(8,128)(2,1)}, u32[]{:S(2)}) copy-start(bf16[1,256,16,128]{3,2,1,0:T(8,128)(2,1)} %param.8) | copy-start | bytes 3145732
  28.0 9.2 %copy-start.5 = (s32[1,9]{1,0:T(1,128)S(1)}, s32[1,9]{1,0:T(1,128)}, u32[]{:S(2)}) copy-start(s32[1,9]{1,0:T(1,128)} %copy-done.4) | copy-start | bytes 112
  28.0 9.2 %copy-start.7 = (s32[1,9]{1,0:T(1,128)S(1)}, s32[1,9]{1,0:T(1,128)}, u32[]{:S(2)}) copy-start(s32[1,9]{1,0:T(1,128)} %copy-done.6) | copy-start | bytes 112
  28.0 9.2 %copy-start.9 = (s32[1,9]{1,0:T(1,128)S(1)}, s32[1,9]{1,0:T(1,128)}, u32[]{:S(2)}) copy-start(s32[1,9]{1,0:T(1,128)} %copy-done.8) | copy-start | bytes 112
  40.5 47.3 %collective-permute-start.10 = (bf16[3,2,256,128]{3,2,1,0:T(8,128)(2,1)S(1)}, bf16[3,2,256,128]{3,2,1,0:T(8,128)(2,1)S(1)}, u32[]{:S(2)}, u32[]{:S(2)}) collective-permute-start(bf16[3,2,256,128]{3,2,1,0:T(8,128)(2,1)S(1)} %get-tuple-element.50), channel_id=1, source_target_pairs={{0,8},{4,12},{8,0},{12,4},{1,9},{5,13},{9,1},{13,5},{2,10},{6,14},... | collective-permute-start | bytes 1179656 | tf_op jit(solution)/shard_map/ppermute | solution.py:417
  40.8 63.5 %collective-permute-start.11 = (bf16[3,2,256,128]{3,2,1,0:T(8,128)(2,1)S(1)}, bf16[3,2,256,128]{3,2,1,0:T(8,128)(2,1)S(1)}, u32[]{:S(2)}, u32[]{:S(2)}) collective-permute-start(bf16[3,2,256,128]{3,2,1,0:T(8,128)(2,1)S(1)} %get-tuple-element.51), channel_id=1, source_target_pairs={{0,12},{4,0},{8,4},{12,8},{1,13},{5,1},{9,5},{13,9},{2,14},{6,2},{... | collective-permute-start | bytes 1179656 | tf_op jit(solution)/shard_map/ppermute | solution.py:417
  75.9 28.3 %collective-permute-start.12 = (bf16[3,2,256,128]{3,2,1,0:T(8,128)(2,1)S(1)}, bf16[3,2,256,128]{3,2,1,0:T(8,128)(2,1)S(1)}, u32[]{:S(2)}, u32[]{:S(2)}) collective-permute-start(bf16[3,2,256,128]{3,2,1,0:T(8,128)(2,1)S(1)} %get-tuple-element.52), channel_id=1, source_target_pairs={{0,4},{4,8},{8,12},{12,0},{1,5},{5,9},{9,13},{13,1},{2,6},{6,10},{... | collective-permute-start | bytes 1179656 | tf_op jit(solution)/shard_map/ppermute | solution.py:417
  76.0 11.8 %copy-start.10 = (s32[1,2]{1,0:T(1,128)S(1)}, s32[1,2]{1,0:T(1,128)}, u32[]{:S(2)}) copy-start(s32[1,2]{1,0:T(1,128)} %slot_ref.1) | copy-start | bytes 28
  76.0 11.8 %copy-start.11 = (s32[1,2]{1,0:T(1,128)S(1)}, s32[1,2]{1,0:T(1,128)}, u32[]{:S(2)}) copy-start(s32[1,2]{1,0:T(1,128)} %owner_ref.1) | copy-start | bytes 28
  81.9 28.4 %collective-permute-start.7 = (bf16[2,2,256,128]{3,2,1,0:T(8,128)(2,1)S(1)}, bf16[2,2,256,128]{3,2,1,0:T(8,128)(2,1)S(1)}, u32[]{:S(2)}, u32[]{:S(2)}) collective-permute-start(bf16[2,2,256,128]{3,2,1,0:T(8,128)(2,1)S(1)} %get-tuple-element.47), channel_id=1, source_target_pairs={{0,8},{4,12},{8,0},{12,4},{1,9},{5,13},{9,1},{13,5},{2,10},{6,14},... | collective-permute-start | bytes 786440 | tf_op jit(solution)/shard_map/ppermute | solution.py:417
  85.7 28.9 %collective-permute-start.8 = (bf16[2,2,256,128]{3,2,1,0:T(8,128)(2,1)S(1)}, bf16[2,2,256,128]{3,2,1,0:T(8,128)(2,1)S(1)}, u32[]{:S(2)}, u32[]{:S(2)}) collective-permute-start(bf16[2,2,256,128]{3,2,1,0:T(8,128)(2,1)S(1)} %get-tuple-element.48), channel_id=1, source_target_pairs={{0,12},{4,0},{8,4},{12,8},{1,13},{5,1},{9,5},{13,9},{2,14},{6,2},{... | collective-permute-start | bytes 786440 | tf_op jit(solution)/shard_map/ppermute | solution.py:417
  87.8 26.8 %collective-permute-start.9 = (bf16[2,2,256,128]{3,2,1,0:T(8,128)(2,1)S(1)}, bf16[2,2,256,128]{3,2,1,0:T(8,128)(2,1)S(1)}, u32[]{:S(2)}, u32[]{:S(2)}) collective-permute-start(bf16[2,2,256,128]{3,2,1,0:T(8,128)(2,1)S(1)} %get-tuple-element.49), channel_id=1, source_target_pairs={{0,4},{4,8},{8,12},{12,0},{1,5},{5,9},{9,13},{13,1},{2,6},{6,10},{... | collective-permute-start | bytes 786440 | tf_op jit(solution)/shard_map/ppermute | solution.py:417

commit v3 on v2

--- a/solution.py
+++ b/solution.py
@@ -24,8 +24,8 @@
     sources, refs = refs[:6], refs[6:]
     num_blk = refs[0].shape[1] // 2
     count_ref, asked, refs = refs[0], refs[1 : 1 + num_blk], refs[1 + num_blk :]
-    fresh_ref, refs = refs[0], refs[1:]
-    held, (table_ref, used_ref, counted_ref, load_sems, store_sem) = refs[:6], refs[6:]
+    fresh, refs = refs[: len(to)], refs[len(to) :]
+    held, (table_ref, used_ref, counted_ref, load_sems, store_sems) = refs[:6], refs[6:]
     loads = [
         pltpu.make_async_copy(source, target, load_sems.at[i])
         for i, (source, target) in enumerate(zip(sources, held))
@@ -41,14 +41,17 @@
             table_ref[owner, k] = 0
     for load in loads:
         load.wait()
-    target = lax.rem(me + to, num_blk)
-    chosen = jnp.int32(0)
-    for b in range(write_owner_ref.shape[1]):
-        chosen = jnp.where(write_owner_ref[0, b] == target, b, chosen)
-    block_rows = fresh_ref.shape[2]
-    rows = pl.ds(pl.multiple_of(chosen * block_rows, block_rows), block_rows)
-    store = pltpu.make_async_copy(new_ref.at[:, rows], fresh_ref.at[0], store_sem)
-    store.start()
+    stores = []
+    for i, (d, out) in enumerate(zip(to, fresh)):
+        target = lax.rem(me + d, num_blk)
+        chosen = jnp.int32(0)
+        for b in range(write_owner_ref.shape[1]):
+            chosen = jnp.where(write_owner_ref[0, b] == target, b, chosen)
+        block_rows = out.shape[2]
+        rows = pl.ds(pl.multiple_of(chosen * block_rows, block_rows), block_rows)
+        stores.append(pltpu.make_async_copy(new_ref.at[:, rows], out.at[0], store_sems.at[i]))
+    for store in stores:
+        store.start()
 
     def step(j, carry):
         owner = owner_ref[0, j]
@@ -72,7 +75,8 @@
             chosen = jnp.where(goes, b, chosen)
         asked[d][0, capacity] = slot
         count_ref[0, num_blk + d] = chosen
-    store.wait()
+    for store in stores:
+        store.wait()
 
 
 def prepare(
@@ -86,9 +90,9 @@
         functools.partial(prepare_kernel, capacity, to),
         out_shape=[jax.ShapeDtypeStruct((1, 2 * num_blk), jnp.int32)]
         + [row] * num_blk
-        + [block],
+        + [block] * len(to),
         in_specs=[HBM] * 6,
-        out_specs=[SMEM] * (num_blk + 1) + [HBM],
+        out_specs=[SMEM] * (num_blk + 1) + [HBM] * len(to),
         scratch_shapes=[pltpu.SMEM(operand.shape, operand.dtype) for operand in operands[:5]]
         + [
             pltpu.VMEM(new_rows.shape, new_rows.dtype),
@@ -96,11 +100,11 @@
             pltpu.SMEM((num_blk,), jnp.int32),
             pltpu.SMEM((num_blk,), jnp.int32),
             pltpu.SemaphoreType.DMA((6,)),
-            pltpu.SemaphoreType.DMA,
+            pltpu.SemaphoreType.DMA((len(to),)),
         ],
         compiler_params=pltpu.CompilerParams(vmem_limit_bytes=WHOLE_LIMIT),
     )(*operands)
-    return results[0], results[1:-1], results[-1]
+    return results[0], results[1 : num_blk + 1], results[num_blk + 1 :]
 
 
 def gather_kernel(plan, count, block_rows, direct, whole, count_ref, *refs):
@@ -416,8 +420,8 @@
     def shift(array, d):
         return lax.ppermute(array, "blk", [(i, (i + d) % num_blk) for i in range(num_blk)])
 
-    ahead = num_blk - shifts[0]
-    counts, asks, farthest = prepare(
+    ahead = shifts[:2]
+    counts, asks, early = prepare(
         prefix_slot,
         prefix_owner,
         prefix_len,
@@ -425,11 +429,11 @@
         write_owner,
         new_rows,
         block_tok * kv_dev,
-        ahead,
+        tuple(num_blk - d for d in ahead),
         capacity,
         num_blk,
     )
-    farthest = shift(farthest, ahead)
+    early = [shift(block, num_blk - d) for d, block in zip(ahead, early)]
     asked = {d: shift(asks[d], d) for d in shifts}
     rows = [asked[d] for d in shifts]
 
@@ -444,7 +448,7 @@
             pool_rows,
             new_rows,
             tuple(
-                (shifts.index(d), start, size, num_blk - d if first and d != shifts[0] else None)
+                (shifts.index(d), start, size, num_blk - d if first and d not in ahead else None)
                 for d, start, size in plan
             ),
             after,
@@ -457,7 +461,7 @@
     loaded = load(plans[0], True)
     arrived = [send(plans[0], loaded)]
     local, new_pool = gather(
-        counts, [asks[0]], pool_rows, new_rows, ((0, 0, capacity, None),), [loaded[0], farthest], whole=True
+        counts, [asks[0]], pool_rows, new_rows, ((0, 0, capacity, None),), [loaded[0], *early], whole=True
     )
     step = functools.partial(attend, counts, queries[0], kv_dev=kv_dev, block_tok=block_tok)
     state, _ = step([local], ((0, 0, capacity),), new_rows=new_rows)
@@ -487,7 +491,7 @@
                 write_slot,
                 [asked[num_blk - d] for d in shifts],
                 new_rows,
-                [farthest, *arrived[0][1:]],
+                [*early, *arrived[0][len(early) :]],
                 new_pool,
                 capacity,
             )

time: 121 us -> 121 us (level); the launches traced: 120 us -> 121 us
    ppermute x13 -> x14, waiting for transfers between devices: 56.1 us -> 56.4 us  [shift(): lax.ppermute(array, 'blk', [(i, (i + d) % num_blk) for i in range(num_blk)])]
    ppermute x13 -> x14, starting transfers between devices: 19.2 us -> 19.3 us  [shift(): lax.ppermute(array, 'blk', [(i, (i + d) % num_blk) for i in range(num_blk)])]
  transfers between devices with their start and end apart: 13 -> 14, of which waited for: 4 -> 5; matrix products, arithmetic and copies ran while one was open for 0% -> 0% of each run, Pallas kernels for 28% -> 28%
where the time goes in v3:
time: 121 us
  waiting for transfers between devices  56.4 us (47%)
  Pallas kernels  41.8 us (35%)
  starting transfers between devices  19.3 us (16%)
  between operations  1.67 us (1%)
  local copies, waits for them, and re-layouts  1.57 us (1%)
    ppermute x14, waiting for transfers between devices, shift(): lax.ppermute(array, 'blk', [(i, (i + d) % num_blk) for i in range(num_blk)])  56.4 us
    pallas_call x4, Pallas kernels, attend(): pl.pallas_call(functools.partial(attend_kernel, spans, len(relay), len(af...  26.9 us
    ppermute x14, starting transfers between devices, shift(): lax.ppermute(array, 'blk', [(i, (i + d) % num_blk) for i in range(num_blk)])  19.3 us
    pallas_call x3, Pallas kernels, gather(): pl.pallas_call(functools.partial(gather_kernel, plan, len(asked), pool.sh...  10 us
    pallas_call x1, Pallas kernels, prepare(): pl.pallas_call(functools.partial(prepare_kernel, capacity, to), out_shape...  2.49 us
  transfers between devices with their start and end apart: 14, of which 5 were waited for; matrix products, arithmetic and copies ran while one was open for 0% of the time, Pallas kernels for 28%

profile of v3, /device:TPU:14, one launch (start us, length us, event | category | flops | bytes accessed | tf_op | source)
XLA Modules:
  0.0 120.8 jit_solution(13841834676170128270)
XLA Ops:
  0.6 0.0 copy-start.1
  0.6 0.0 copy-start
  1.4 2.5 %shard_map.95 = (s32[1,8]{1,0:T(1,128)}, s32[1,9]{1,0:T(1,128)}, s32[1,9]{1,0:T(1,128)}, s32[1,9]{1,0:T(1,128)}, s32[1,9]{1,0:T(1,128)}, /*index=5*/bf16[1,2,256...) custom-call(s32[1,32]{1,0:T(1,128)} %refs_0_.1, s32[1,32]{1,0:T(1,128)} %refs_1_.1, s32[1]{0:T(128)S(6)} %copy.18.refs_2_, ...), custom_call_target="tpu_custom_call" | custom-call | tf_op jit(solution)/shard_map/pallas_call | solution.py:89
  3.9 0.0 copy-start.3
  4.0 0.0 copy-start.12
  4.0 2.7 %collective-permute-start.3 = (bf16[1,2,256,128]{3,2,1,0:T(8,128)(2,1)}, bf16[1,2,256,128]{3,2,1,0:T(8,128)(2,1)S(1)}, u32[]{:S(2)}, u32[]{:S(2)}) collective-permute-start(bf16[1,2,256,128]{3,2,1,0:T(8,128)(2,1)} %get-tuple-element.38), channel_id=1, source_target_pairs={{0,8},{4,12},{8,0},{12,4},{1,9},{5,13},{9,1},{13,5},{2,10},{6,14},... | collective-permute-start | bytes 393224 | tf_op jit(solution)/shard_map/ppermute | solution.py:421
  6.6 0.4 collective-permute-start.4
  7.1 0.3 collective-permute-start
  7.4 2.5 %collective-permute-start.1 = (s32[1,9]{1,0:T(1,128)}, s32[1,9]{1,0:T(1,128)S(1)}, u32[]{:S(2)}, u32[]{:S(2)}) collective-permute-start(s32[1,9]{1,0:T(1,128)} %get-tuple-element.35), channel_id=1, source_target_pairs={{0,4},{4,8},{8,12},{12,0},{1,5},{5,9},{9,13},{13,1},{2,6},{6,10},{... | collective-permute-start | bytes 116 | tf_op jit(solution)/shard_map/ppermute | solution.py:421
  9.9 0.2 collective-permute-start.2
  10.1 5.1 %collective-permute-done.refs_0_ = s32[1,9]{1,0:T(1,128)S(1)} collective-permute-done((s32[1,9]{1,0:T(1,128)}, s32[1,9]{1,0:T(1,128)S(1)}, u32[]{:S(2)}, u32[]{:S(2)}) %collective-permute-start) | collective-permute-done | bytes 68 | tf_op jit(solution)/shard_map/ppermute | solution.py:421
  15.3 0.0 collective-permute-done.1.refs_1_.refs_2_
  15.3 0.0 collective-permute-done.2.refs_2_.refs_1_
  15.3 0.0 copy-start.8
  15.3 0.5 copy-done.4
  15.8 0.0 copy-done.8
  15.8 2.9 %shard_map.96 = (bf16[3,2,256,128]{3,2,1,0:T(8,128)(2,1)}, bf16[3,2,256,128]{3,2,1,0:T(8,128)(2,1)}, bf16[4,2,256,128]{3,2,1,0:T(8,128)(2,1)}) custom-call(s32[1,8]{1,0:T(1,128)} %get-tuple-element.32.count_ref, s32[1,9]{1,0:T(1,128)} %copy-done.4, s32[1,9]{1,0:T(1,128)} %copy-done.6, s32[1,9]{1,0:T(1,128)} %copy-done.8, bf16[24,2,256,128]{3,2,1,0:T(8,128)(2,1)} %bitcast.5, ...), custom_call_target="tpu_custom_call" | custom-call | bytes 2621440 | tf_op jit(solution)/shard_map/pallas_call | solution.py:154
  18.7 2.6 %collective-permute-start.7 = (bf16[4,2,256,128]{3,2,1,0:T(8,128)(2,1)}, bf16[4,2,256,128]{3,2,1,0:T(8,128)(2,1)S(1)}, u32[]{:S(2)}, u32[]{:S(2)}) collective-permute-start(bf16[4,2,256,128]{3,2,1,0:T(8,128)(2,1)} %get-tuple-element.43), channel_id=1, source_target_pairs={{0,4},{4,8},{8,12},{12,0},{1,5},{5,9},{9,13},{13,1},{2,6},{6,10},{... | collective-permute-start | bytes 1572872 | tf_op jit(solution)/shard_map/ppermute | solution.py:421
  21.3 1.0 collective-permute-start.5
  22.3 1.8 %collective-permute-start.6 = (bf16[3,2,256,128]{3,2,1,0:T(8,128)(2,1)}, bf16[3,2,256,128]{3,2,1,0:T(8,128)(2,1)S(1)}, u32[]{:S(2)}, u32[]{:S(2)}) collective-permute-start(bf16[3,2,256,128]{3,2,1,0:T(8,128)(2,1)} %get-tuple-element.42), channel_id=1, source_target_pairs={{0,12},{4,0},{8,4},{12,8},{1,13},{5,1},{9,5},{13,9},{2,14},{6,2},{... | collective-permute-start | bytes 1179656 | tf_op jit(solution)/shard_map/ppermute | solution.py:421
  24.1 0.0 collective-permute-done.3.refs_4_
  24.1 0.0 collective-permute-done.4.refs_5_
  24.2 1.0 copy-done.2
  25.1 3.8 %shard_map.97 = (bf16[8,2,256,128]{3,2,1,0:T(8,128)(2,1)S(1)}, bf16[24,2,256,128]{3,2,1,0:T(8,128)(2,1)}) custom-call(s32[1,8]{1,0:T(1,128)S(1)} %copy-done.3, s32[1,9]{1,0:T(1,128)S(1)} %copy-done.12, bf16[24,2,256,128]{3,2,1,0:T(8,128)(2,1)S(1)} %bitcast.6, bf16[2,512,128]{2,1,0:T(8,128)(2,1)S(1)} %bitcast.10, bf16[3,2,256,128]{3,2,1,0:T(8,128)(2,1)S(1)} %copy-done.2, ...), custom_call_target="tpu_custom_call" | custom-call | bytes 8388608 | tf_op jit(solution)/shard_map/pallas_call | solution.py:154
  29.0 9.0 %shard_map.98 = (bf16[2,2048,128]{2,1,0:T(8,128)(2,1)S(1)}, f32[2,128,2048]{2,1,0:T(8,128)S(1)}, f32[2,8,2048]{2,1,0:T(8,128)S(1)}) custom-call(s32[1,8]{1,0:T(1,128)S(1)} %copy-done.3, bf16[256,16,128]{2,1,0:T(8,128)(2,1)S(1)} %bitcast.14, bf16[8,2,256,128]{3,2,1,0:T(8,128)(2,1)S(1)} %get-tuple-element.40.refs_0_, bf16[2,512,128]{2,1,0:T(8,128)(2,1)S(1)} %bitcast.11), custom_call_target="tpu_custom_call" | custom-call | flops 2684354560 | bytes 9699328 | tf_op jit(solution)/shard_map/pallas_call | solution.py:382
  38.0 3.3 %shard_map.99 = (bf16[3,2,256,128]{3,2,1,0:T(8,128)(2,1)S(1)}, bf16[3,2,256,128]{3,2,1,0:T(8,128)(2,1)S(1)}, bf16[3,2,256,128]{3,2,1,0:T(8,128)(2,1)S(1)}, bf16[...) custom-call(s32[1,8]{1,0:T(1,128)S(1)} %copy-done.3, ...), custom_call_target="tpu_custom_call" | custom-call | bytes 3932160 | tf_op jit(solution)/shard_map/pallas_call | solution.py:154
  41.3 0.6 collective-permute-start.11
  41.9 1.8 %collective-permute-start.12 = (bf16[3,2,256,128]{3,2,1,0:T(8,128)(2,1)S(1)}, bf16[3,2,256,128]{3,2,1,0:T(8,128)(2,1)S(1)}, u32[]{:S(2)}, u32[]{:S(2)}) collective-permute-start(bf16[3,2,256,128]{3,2,1,0:T(8,128)(2,1)S(1)} %get-tuple-element.53), channel_id=1, source_target_pairs={{0,12},{4,0},{8,4},{12,8},{1,13},{5,1},{9,5},{13,9},{2,14},{6,2},{... | collective-permute-start | bytes 1179656 | tf_op jit(solution)/shard_map/ppermute | solution.py:421
  43.7 32.4 %collective-permute-done.5.refs_0_ = bf16[3,2,256,128]{3,2,1,0:T(8,128)(2,1)S(1)} collective-permute-done((bf16[3,2,256,128]{3,2,1,0:T(8,128)(2,1)}, bf16[3,2,256,128]{3,2,1,0:T(8,128)(2,1)S(1)}, u32[]{:S(2)}, u32[]{:S(2)}) %collective-permute-start.5) | collective-permute-done | bytes 393248 | tf_op jit(solution)/shard_map/ppermute | solution.py:421
  76.1 0.0 collective-permute-start.13
  76.1 0.0 collective-permute-done.6.refs_1_
  76.1 0.0 collective-permute-done.7.refs_2_.refs_6_
  76.1 0.0 copy-start.10
  76.1 0.0 copy-start.11
  76.1 6.4 %shard_map.100 = (f32[2,128,2048]{2,1,0:T(8,128)S(1)}, f32[2,8,2048]{2,1,0:T(8,128)S(1)}, bf16[2,2,256,128]{3,2,1,0:T(8,128)(2,1)S(1)}, bf16[2,2,256,128]{3,2,1,0:T(8,128)(2,1)S(1)}, bf16[2,2,256,128]{3,2,1,0:T(8,128)(2,1)S(1)}) custom-call(s32[1,8]{1,0:T(1,128)S(1)} %copy-done.3, ...), custom_call_target="tpu_custom_call", output_to_operand_aliasing={{2}: (7, {}), {3}: (8, {}), {4}: (9, {})} | custom-call | flops 2415919104 | bytes 9568256 | tf_op jit(solution)/shard_map/pallas_call | solution.py:382
  82.6 3.9 %collective-permute-start.10 = (bf16[2,2,256,128]{3,2,1,0:T(8,128)(2,1)S(1)}, bf16[2,2,256,128]{3,2,1,0:T(8,128)(2,1)S(1)}, u32[]{:S(2)}, u32[]{:S(2)}) collective-permute-start(bf16[2,2,256,128]{3,2,1,0:T(8,128)(2,1)S(1)} %get-tuple-element.51), channel_id=1, source_target_pairs={{0,4},{4,8},{8,12},{12,0},{1,5},{5,9},{9,13},{13,1},{2,6},{6,10},{... | collective-permute-start | bytes 786440 | tf_op jit(solution)/shard_map/ppermute | solution.py:421
  86.4 0.5 collective-permute-start.8
  87.0 0.0 collective-permute-done.11.refs_0_
  87.0 1.0 collective-permute-start.9
  88.0 0.0 copy-done.11
  88.0 2.4 %shard_map.101 = (bf16[24,2,256,128]{3,2,1,0:T(8,128)(2,1)}, s32[1,1]{1,0:T(1,128)}) custom-call(s32[1,2]{1,0:T(1,128)S(1)} %copy-done.11, s32[1,2]{1,0:T(1,128)S(1)} %copy-done.10, s32[1,9]{1,0:T(1,128)S(1)} %copy-done.5, s32[1,9]{1,0:T(1,128)S(1)} %copy-done.9, s32[1,9]{1,0:T(1,128)S(1)} %copy-done.7, ...), custom_call_target="tpu_custom_call", output_to_operand_aliasing={{0}: (9, {})} | custom-call | bytes 1048576 | tf_op jit(solution)/shard_map/pallas_call | solution.py:193
  90.4 14.3 %collective-permute-done.12.refs_1_ = bf16[3,2,256,128]{3,2,1,0:T(8,128)(2,1)S(1)} collective-permute-done((bf16[3,2,256,128]{3,2,1,0:T(8,128)(2,1)S(1)}, bf16[3,2,256,128]{3,2,1,0:T(8,128)(2,1)S(1)}, u32[]{:S(2)}, u32[]{:S(2)}) %collective-permute-start.12) | collective-permute-done | bytes 393248 | tf_op jit(solution)/shard_map/ppermute | solution.py:421
  104.7 0.0 collective-permute-done.13.refs_2_
  104.7 6.5 %shard_map.102 = (f32[2,128,2048]{2,1,0:T(8,128)S(1)}, f32[2,8,2048]{2,1,0:T(8,128)S(1)}) custom-call(s32[1,8]{1,0:T(1,128)S(1)} %copy-done.3, bf16[2,2048,128]{2,1,0:T(8,128)(2,1)S(1)} %get-tuple-element.41.q_ref, bf16[3,2,256,128]{3,2,1,0:T(8,128)(2,1)S(1)} %collective-permute-done.11.refs_0_, ...), custom_call_target="tpu_custom_call" | custom-call | flops 2415919104 | bytes 9568256 | tf_op jit(solution)/shard_map/pallas_call | solution.py:382
  111.2 0.0 collective-permute-done.10.refs_2_
  111.3 2.8 %collective-permute-done.8.refs_0_ = bf16[2,2,256,128]{3,2,1,0:T(8,128)(2,1)S(1)} collective-permute-done((bf16[2,2,256,128]{3,2,1,0:T(8,128)(2,1)S(1)}, bf16[2,2,256,128]{3,2,1,0:T(8,128)(2,1)S(1)}, u32[]{:S(2)}, u32[]{:S(2)}) %collective-permute-start.8) | collective-permute-done | bytes 262176 | tf_op jit(solution)/shard_map/ppermute | solution.py:421
  114.1 1.8 %collective-permute-done.9.refs_1_ = bf16[2,2,256,128]{3,2,1,0:T(8,128)(2,1)S(1)} collective-permute-done((bf16[2,2,256,128]{3,2,1,0:T(8,128)(2,1)S(1)}, bf16[2,2,256,128]{3,2,1,0:T(8,128)(2,1)S(1)}, u32[]{:S(2)}, u32[]{:S(2)}) %collective-permute-start.9) | collective-permute-done | bytes 262176 | tf_op jit(solution)/shard_map/ppermute | solution.py:421
  115.9 5.0 %shard_map.103 = bf16[256,16,128]{2,1,0:T(8,128)(2,1)} custom-call(s32[1,8]{1,0:T(1,128)S(1)} %copy-done.3, bf16[2,2048,128]{2,1,0:T(8,128)(2,1)S(1)} %get-tuple-element.41.q_ref, bf16[2,2,256,128]{3,2,1,0:T(8,128)(2,1)S(1)} %collective-permute-done.8.refs_0_, bf16[2,2,256,128]{3,2,1,0:T(8,128)(2,1)S(1)} %collective-permute-done.9.refs_1_, ...), custom_call_target="tpu_custom_call" | custom-call | flops 1610612736 | bytes 9175040 | tf_op jit(solution)/shard_map/pallas_call | solution.py:382
  (17 shorter events, 0.0 us)
Async XLA Ops:
  0.6 23.5 %copy-start.1 = (bf16[2,1,256,2,128]{4,3,2,1,0:T(2,128)(2,1)S(1)}, bf16[2,1,256,2,128]{4,3,2,1,0:T(2,128)(2,1)}, u32[]{:S(2)}) copy-start(bf16[2,1,256,2,128]{4,3,2,1,0:T(2,128)(2,1)} %param.9) | copy-start | bytes 786436
  0.6 23.5 %copy-start = (bf16[24,2,128,2,128]{4,3,2,1,0:T(2,128)(2,1)S(1)}, bf16[24,2,128,2,128]{4,3,2,1,0:T(2,128)(2,1)}, u32[]{:S(2)}) copy-start(bf16[24,2,128,2,128]{4,3,2,1,0:T(2,128)(2,1)} %param.10) | copy-start | bytes 9437188
  3.9 20.2 %copy-start.3 = (s32[1,8]{1,0:T(1,128)S(1)}, s32[1,8]{1,0:T(1,128)}, u32[]{:S(2)}) copy-start(s32[1,8]{1,0:T(1,128)} %get-tuple-element.32.count_ref) | copy-start | bytes 100
  4.0 20.2 %copy-start.12 = (s32[1,9]{1,0:T(1,128)S(1)}, s32[1,9]{1,0:T(1,128)}, u32[]{:S(2)}) copy-start(s32[1,9]{1,0:T(1,128)} %get-tuple-element.33.refs_0_) | copy-start | bytes 112
  4.0 20.1 %collective-permute-start.3 = (bf16[1,2,256,128]{3,2,1,0:T(8,128)(2,1)}, bf16[1,2,256,128]{3,2,1,0:T(8,128)(2,1)S(1)}, u32[]{:S(2)}, u32[]{:S(2)}) collective-permute-start(bf16[1,2,256,128]{3,2,1,0:T(8,128)(2,1)} %get-tuple-element.38), channel_id=1, source_target_pairs={{0,8},{4,12},{8,0},{12,4},{1,9},{5,13},{9,1},{13,5},{2,10},{6,14},... | collective-permute-start | bytes 393224 | tf_op jit(solution)/shard_map/ppermute | solution.py:421
  6.6 17.5 %collective-permute-start.4 = (bf16[1,2,256,128]{3,2,1,0:T(8,128)(2,1)}, bf16[1,2,256,128]{3,2,1,0:T(8,128)(2,1)S(1)}, u32[]{:S(2)}, u32[]{:S(2)}) collective-permute-start(bf16[1,2,256,128]{3,2,1,0:T(8,128)(2,1)} %get-tuple-element.39), channel_id=1, source_target_pairs={{0,12},{4,0},{8,4},{12,8},{1,13},{5,1},{9,5},{13,9},{2,14},{6,2},{... | collective-permute-start | bytes 393224 | tf_op jit(solution)/shard_map/ppermute | solution.py:421
  7.1 8.2 %collective-permute-start = (s32[1,9]{1,0:T(1,128)}, s32[1,9]{1,0:T(1,128)S(1)}, u32[]{:S(2)}, u32[]{:S(2)}) collective-permute-start(s32[1,9]{1,0:T(1,128)} %get-tuple-element.34), channel_id=1, source_target_pairs={{0,8},{4,12},{8,0},{12,4},{1,9},{5,13},{9,1},{13,5},{2,10},{6,14},... | collective-permute-start | bytes 116 | tf_op jit(solution)/shard_map/ppermute | solution.py:421
  7.4 7.9 %collective-permute-start.1 = (s32[1,9]{1,0:T(1,128)}, s32[1,9]{1,0:T(1,128)S(1)}, u32[]{:S(2)}, u32[]{:S(2)}) collective-permute-start(s32[1,9]{1,0:T(1,128)} %get-tuple-element.35), channel_id=1, source_target_pairs={{0,4},{4,8},{8,12},{12,0},{1,5},{5,9},{9,13},{13,1},{2,6},{6,10},{... | collective-permute-start | bytes 116 | tf_op jit(solution)/shard_map/ppermute | solution.py:421
  9.9 5.4 %collective-permute-start.2 = (s32[1,9]{1,0:T(1,128)}, s32[1,9]{1,0:T(1,128)S(1)}, u32[]{:S(2)}, u32[]{:S(2)}) collective-permute-start(s32[1,9]{1,0:T(1,128)} %get-tuple-element.36), channel_id=1, source_target_pairs={{0,12},{4,0},{8,4},{12,8},{1,13},{5,1},{9,5},{13,9},{2,14},{6,2},{... | collective-permute-start | bytes 116 | tf_op jit(solution)/shard_map/ppermute | solution.py:421
  15.3 0.5 copy-start.4
  15.3 0.5 copy-start.6
  15.3 0.5 copy-start.8
  18.7 57.4 %collective-permute-start.7 = (bf16[4,2,256,128]{3,2,1,0:T(8,128)(2,1)}, bf16[4,2,256,128]{3,2,1,0:T(8,128)(2,1)S(1)}, u32[]{:S(2)}, u32[]{:S(2)}) collective-permute-start(bf16[4,2,256,128]{3,2,1,0:T(8,128)(2,1)} %get-tuple-element.43), channel_id=1, source_target_pairs={{0,4},{4,8},{8,12},{12,0},{1,5},{5,9},{9,13},{13,1},{2,6},{6,10},{... | collective-permute-start | bytes 1572872 | tf_op jit(solution)/shard_map/ppermute | solution.py:421
  21.3 54.8 %collective-permute-start.5 = (bf16[3,2,256,128]{3,2,1,0:T(8,128)(2,1)}, bf16[3,2,256,128]{3,2,1,0:T(8,128)(2,1)S(1)}, u32[]{:S(2)}, u32[]{:S(2)}) collective-permute-start(bf16[3,2,256,128]{3,2,1,0:T(8,128)(2,1)} %get-tuple-element.37.refs_3_), channel_id=1, source_target_pairs={{0,8},{4,12},{8,0},{12,4},{1,9},{5,13},{9,1},{13,5},{2,10},{6,14},... | collective-permute-start | bytes 1179656 | tf_op jit(solution)/shard_map/ppermute | solution.py:421
  22.3 53.8 %collective-permute-start.6 = (bf16[3,2,256,128]{3,2,1,0:T(8,128)(2,1)}, bf16[3,2,256,128]{3,2,1,0:T(8,128)(2,1)S(1)}, u32[]{:S(2)}, u32[]{:S(2)}) collective-permute-start(bf16[3,2,256,128]{3,2,1,0:T(8,128)(2,1)} %get-tuple-element.42), channel_id=1, source_target_pairs={{0,12},{4,0},{8,4},{12,8},{1,13},{5,1},{9,5},{13,9},{2,14},{6,2},{... | collective-permute-start | bytes 1179656 | tf_op jit(solution)/shard_map/ppermute | solution.py:421
  24.1 1.0 copy-start.2
  25.1 3.9 %copy-start.13 = (bf16[1,256,16,128]{3,2,1,0:T(8,128)(2,1)S(1)}, bf16[1,256,16,128]{3,2,1,0:T(8,128)(2,1)}, u32[]{:S(2)}) copy-start(bf16[1,256,16,128]{3,2,1,0:T(8,128)(2,1)} %param.8) | copy-start | bytes 3145732
  29.0 9.0 %copy-start.5 = (s32[1,9]{1,0:T(1,128)S(1)}, s32[1,9]{1,0:T(1,128)}, u32[]{:S(2)}) copy-start(s32[1,9]{1,0:T(1,128)} %copy-done.4) | copy-start | bytes 112
  29.0 9.0 %copy-start.7 = (s32[1,9]{1,0:T(1,128)S(1)}, s32[1,9]{1,0:T(1,128)}, u32[]{:S(2)}) copy-start(s32[1,9]{1,0:T(1,128)} %copy-done.6) | copy-start | bytes 112
  29.0 9.0 %copy-start.9 = (s32[1,9]{1,0:T(1,128)S(1)}, s32[1,9]{1,0:T(1,128)}, u32[]{:S(2)}) copy-start(s32[1,9]{1,0:T(1,128)} %copy-done.8) | copy-start | bytes 112
  41.3 45.7 %collective-permute-start.11 = (bf16[3,2,256,128]{3,2,1,0:T(8,128)(2,1)S(1)}, bf16[3,2,256,128]{3,2,1,0:T(8,128)(2,1)S(1)}, u32[]{:S(2)}, u32[]{:S(2)}) collective-permute-start(bf16[3,2,256,128]{3,2,1,0:T(8,128)(2,1)S(1)} %get-tuple-element.52), channel_id=1, source_target_pairs={{0,8},{4,12},{8,0},{12,4},{1,9},{5,13},{9,1},{13,5},{2,10},{6,14},... | collective-permute-start | bytes 1179656 | tf_op jit(solution)/shard_map/ppermute | solution.py:421
  41.9 62.8 %collective-permute-start.12 = (bf16[3,2,256,128]{3,2,1,0:T(8,128)(2,1)S(1)}, bf16[3,2,256,128]{3,2,1,0:T(8,128)(2,1)S(1)}, u32[]{:S(2)}, u32[]{:S(2)}) collective-permute-start(bf16[3,2,256,128]{3,2,1,0:T(8,128)(2,1)S(1)} %get-tuple-element.53), channel_id=1, source_target_pairs={{0,12},{4,0},{8,4},{12,8},{1,13},{5,1},{9,5},{13,9},{2,14},{6,2},{... | collective-permute-start | bytes 1179656 | tf_op jit(solution)/shard_map/ppermute | solution.py:421
  76.1 28.6 %collective-permute-start.13 = (bf16[3,2,256,128]{3,2,1,0:T(8,128)(2,1)S(1)}, bf16[3,2,256,128]{3,2,1,0:T(8,128)(2,1)S(1)}, u32[]{:S(2)}, u32[]{:S(2)}) collective-permute-start(bf16[3,2,256,128]{3,2,1,0:T(8,128)(2,1)S(1)} %get-tuple-element.54), channel_id=1, source_target_pairs={{0,4},{4,8},{8,12},{12,0},{1,5},{5,9},{9,13},{13,1},{2,6},{6,10},{... | collective-permute-start | bytes 1179656 | tf_op jit(solution)/shard_map/ppermute | solution.py:421
  76.1 11.9 %copy-start.10 = (s32[1,2]{1,0:T(1,128)S(1)}, s32[1,2]{1,0:T(1,128)}, u32[]{:S(2)}) copy-start(s32[1,2]{1,0:T(1,128)} %slot_ref.1) | copy-start | bytes 28
  76.1 11.9 %copy-start.11 = (s32[1,2]{1,0:T(1,128)S(1)}, s32[1,2]{1,0:T(1,128)}, u32[]{:S(2)}) copy-start(s32[1,2]{1,0:T(1,128)} %owner_ref.1) | copy-start | bytes 28
  82.6 28.7 %collective-permute-start.10 = (bf16[2,2,256,128]{3,2,1,0:T(8,128)(2,1)S(1)}, bf16[2,2,256,128]{3,2,1,0:T(8,128)(2,1)S(1)}, u32[]{:S(2)}, u32[]{:S(2)}) collective-permute-start(bf16[2,2,256,128]{3,2,1,0:T(8,128)(2,1)S(1)} %get-tuple-element.51), channel_id=1, source_target_pairs={{0,4},{4,8},{8,12},{12,0},{1,5},{5,9},{9,13},{13,1},{2,6},{6,10},{... | collective-permute-start | bytes 786440 | tf_op jit(solution)/shard_map/ppermute | solution.py:421
  86.4 27.6 %collective-permute-start.8 = (bf16[2,2,256,128]{3,2,1,0:T(8,128)(2,1)S(1)}, bf16[2,2,256,128]{3,2,1,0:T(8,128)(2,1)S(1)}, u32[]{:S(2)}, u32[]{:S(2)}) collective-permute-start(bf16[2,2,256,128]{3,2,1,0:T(8,128)(2,1)S(1)} %get-tuple-element.49), channel_id=1, source_target_pairs={{0,8},{4,12},{8,0},{12,4},{1,9},{5,13},{9,1},{13,5},{2,10},{6,14},... | collective-permute-start | bytes 786440 | tf_op jit(solution)/shard_map/ppermute | solution.py:421
  87.0 28.9 %collective-permute-start.9 = (bf16[2,2,256,128]{3,2,1,0:T(8,128)(2,1)S(1)}, bf16[2,2,256,128]{3,2,1,0:T(8,128)(2,1)S(1)}, u32[]{:S(2)}, u32[]{:S(2)}) collective-permute-start(bf16[2,2,256,128]{3,2,1,0:T(8,128)(2,1)S(1)} %get-tuple-element.50), channel_id=1, source_target_pairs={{0,12},{4,0},{8,4},{12,8},{1,13},{5,1},{9,5},{13,9},{2,14},{6,2},{... | collective-permute-start | bytes 786440 | tf_op jit(solution)/shard_map/ppermute | solution.py:421
